TPU v7x, 128 devices: a whole 4x4x4 slice. The times are simulated.
128 devices in a mesh: slab: 32 (over y_hi, x, z), dp: 4 (over y_lo, core).
Axes of the slice: x: 4, y: 4 (y_hi: 2, y_lo: 2; y = y_hi * 2 + y_lo), z: 4, core: 2. Of those that a mesh axis runs over, the one named last changes fastest.
Arguments:
- coarse_in: bfloat16 [4, 2, 64, 4, 8, 256], P('dp', None, 'slab'), may hold values from -6 to 6
- pre_up: bfloat16 [4, 2, 128, 8, 16, 128], P('dp', None, 'slab'), may hold values from -6 to 6
- pre_mid: bfloat16 [4, 2, 128, 8, 16, 128], P('dp', None, 'slab'), may hold values from -6 to 6
- grad_out: bfloat16 [4, 2, 128, 8, 16, 128], P('dp', None, 'slab'), may hold values from -6 to 6
- master: float32 [13824, 128], P(('slab', 'dp')), may hold values from -0.109375 to 0.109375
- moment: float32 [13824, 128], P(('slab', 'dp')), may hold values from -18 to 18
- second: float32 [13824, 128], P(('slab', 'dp')), may hold values from 1 to 30
Outputs:
- coarse_grad: bfloat16 [4, 2, 64, 4, 8, 256], P('dp', None, 'slab')
- new_master: float32 [13824, 128], P(('slab', 'dp'))
- new_moment: float32 [13824, 128], P(('slab', 'dp'))
- new_second: float32 [13824, 128], P(('slab', 'dp'))
All inputs are finite; a program needn't handle non-finite values.
Results may differ from a plain program's by a relative error of at most 0.0075.
Values may be sent and summed in bfloat16 or wider, within the bound.
A program may use at most 128 MiB of HBM per device.

v0:
```python
import jax
import jax.numpy as jnp
from jax import lax
from jax.sharding import PartitionSpec as P

beta_one = 0.9
beta_two = 0.999
adam_step = 10.0
learn_rate = 0.01
adam_eps = 1e-08


def padded_2(shard, sides, width):
    for axis, dim in sides:
        count, length = (lax.axis_size(axis), shard.shape[dim])
        up = [(i, (i + 1) % count) for i in range(count - 1)]
        down = [(j, i) for i, j in up]
        last = lax.slice_in_dim(shard, length - width, length, axis=dim)
        initial = lax.slice_in_dim(shard, 0, width, axis=dim)
        before = lax.ppermute(last, axis, up)
        after = lax.ppermute(initial, axis, down)
        shard = jnp.concatenate([before, shard, after], axis=dim)
    return shard


def from_behind(block, axis, distance):
    devices = range(lax.axis_size(axis))
    route = [(i - distance, i) for i in devices if i - distance in devices]
    return lax.ppermute(block, axis, route)


def correlate(padded, weight):
    samples_here, depth_ext, height, breadth, in_width = padded.shape
    inner_depth = depth_ext - 2
    lateral = jnp.pad(padded, ((0, 0), (0, 0), (1, 1), (1, 1), (0, 0)))
    running = None
    for depth_tap in range(3):
        for row_tap in range(3):
            columns = jnp.concatenate(
                [
                    lateral[
                        :,
                        depth_tap : depth_tap + inner_depth,
                        row_tap : row_tap + height,
                        col_tap : col_tap + breadth,
                        :,
                    ]
                    for col_tap in range(3)
                ],
                axis=-1,
            )
            row_start = (depth_tap * 3 + row_tap) * 3 * in_width
            product_term = jnp.dot(
                columns.reshape(-1, 3 * in_width),
                weight[row_start : row_start + 3 * in_width],
                preferred_element_type=jnp.float32,
            )
            running = product_term if running is None else running + product_term
    return running.reshape(samples_here, inner_depth, height, breadth, weight.shape[1])


def filter_grad(padded, grads):
    samples_here, depth_ext, height, breadth, in_width = padded.shape
    inner_depth = depth_ext - 2
    lateral = jnp.pad(padded, ((0, 0), (0, 0), (1, 1), (1, 1), (0, 0)))
    flat_grads = grads.reshape(-1, grads.shape[-1])
    blocks = []
    for depth_tap in range(3):
        for row_tap in range(3):
            columns = jnp.concatenate(
                [
                    lateral[
                        :,
                        depth_tap : depth_tap + inner_depth,
                        row_tap : row_tap + height,
                        col_tap : col_tap + breadth,
                        :,
                    ]
                    for col_tap in range(3)
                ],
                axis=-1,
            )
            blocks.append(
                lax.dot_general(
                    columns.reshape(-1, 3 * in_width),
                    flat_grads,
                    (((0,), (0,)), ((), ())),
                    preferred_element_type=jnp.float32,
                )
            )
    return jnp.concatenate(blocks, axis=0)


def flipped(weight, in_width):
    out_width = weight.shape[1]
    shaped = weight.reshape(3, 3, 3, in_width, out_width)[::-1, ::-1, ::-1]
    return shaped.transpose(0, 1, 2, 4, 3).reshape(27 * out_width, in_width)


def upconv_back(grad_pad, coarse, weight):
    lateral = jnp.pad(grad_pad, ((0, 0), (0, 0), (1, 0), (1, 0), (0, 0)))
    samples_here, coarse_depth, coarse_rows, coarse_cols, coarse_width = coarse.shape
    fine_width = weight.shape[1]
    slices = []
    for depth_tap in range(3):
        for row_tap in range(3):
            for col_tap in range(3):
                slices.append(
                    lateral[
                        :,
                        depth_tap : depth_tap + 2 * coarse_depth : 2,
                        row_tap : row_tap + 2 * coarse_rows : 2,
                        col_tap : col_tap + 2 * coarse_cols : 2,
                        :,
                    ]
                )
    gathered = jnp.concatenate(slices, axis=-1).reshape(-1, 27 * fine_width)
    turned = (
        weight.reshape(27, coarse_width, fine_width)
        .transpose(0, 2, 1)
        .reshape(27 * fine_width, coarse_width)
    )
    coarse_grad = jnp.dot(gathered, turned, preferred_element_type=jnp.float32).reshape(
        coarse.shape
    )
    filter_part = lax.dot_general(
        coarse.reshape(-1, coarse_width),
        gathered,
        (((0,), (0,)), ((), ())),
        preferred_element_type=jnp.float32,
    )
    filter_part = (
        filter_part.reshape(coarse_width, 27, fine_width)
        .transpose(1, 0, 2)
        .reshape(27 * coarse_width, fine_width)
    )
    return (coarse_grad, filter_part)


def body(coarse_in, pre_up, pre_mid, grad_out, master, moment, second):
    channels = pre_up.shape[-1]
    group_size = pre_up.shape[1]
    shards = lax.all_gather(master.astype(jnp.bfloat16), ("slab", "dp"), axis=0, tiled=True)
    w_one = shards[: 27 * channels]
    w_two = shards[27 * channels : 54 * channels]
    w_up = shards[54 * channels :]
    flip_one = flipped(w_one, channels)
    flip_two = flipped(w_two, channels)
    up_in = pre_up.reshape((-1,) + pre_up.shape[2:])
    mid_in = pre_mid.reshape((-1,) + pre_mid.shape[2:])
    out_in = grad_out.reshape((-1,) + grad_out.shape[2:])
    rim_block = padded_2(jnp.stack([jax.nn.relu(mid_in), out_in]), (("slab", 2),), 1)
    mid_act = rim_block[0]
    out_pad = rim_block[1]
    grad_two = filter_grad(mid_act, out_in)
    back_mid = correlate(out_pad, flip_two)
    mid_grad = jnp.where(mid_in > 0, back_mid, 0.0).astype(jnp.bfloat16)
    inner_rims = padded_2(jnp.stack([jax.nn.relu(up_in), mid_grad]), (("slab", 2),), 1)
    up_act = inner_rims[0]
    mid_grad_pad = inner_rims[1]
    grad_one = filter_grad(up_act, mid_grad)
    back_up = correlate(mid_grad_pad, flip_one)
    up_grad = jnp.where(up_in > 0, back_up, 0.0).astype(jnp.bfloat16)
    previous = from_behind(up_grad[:, -1:], "slab", 1)
    grad_pad = jnp.concatenate([previous, up_grad], axis=1)
    coarse_here = coarse_in.reshape((-1,) + coarse_in.shape[2:])
    coarse_grad, grad_up = upconv_back(grad_pad, coarse_here, w_up)
    coarse_grad = coarse_grad.astype(jnp.bfloat16).reshape(coarse_in.shape)
    partial_value = jnp.concatenate([grad_one, grad_two, grad_up], axis=0)
    totals = lax.psum(partial_value, ("slab", "dp"))
    own_rows = master.shape[0]
    summed = lax.dynamic_slice_in_dim(
        totals, lax.axis_index(("slab", "dp")) * own_rows, own_rows, 0
    )
    mean_grad = summed / float(group_size * lax.axis_size("dp"))
    new_moment = beta_one * moment + (1.0 - beta_one) * mean_grad
    new_second = beta_two * second + (1.0 - beta_two) * mean_grad * mean_grad
    corrected = new_moment / (1.0 - beta_one**adam_step)
    scaled = jnp.sqrt(new_second / (1.0 - beta_two**adam_step)) + adam_eps
    new_master = master - learn_rate * corrected / scaled
    return (coarse_grad, new_master, new_moment, new_second)


def solution(mesh):
    return jax.shard_map(
        body,
        mesh=mesh,
        in_specs=(
            P("dp", None, "slab", None, None, None),
            P("dp", None, "slab", None, None, None),
            P("dp", None, "slab", None, None, None),
            P("dp", None, "slab", None, None, None),
            P(("slab", "dp"), None),
            P(("slab", "dp"), None),
            P(("slab", "dp"), None),
        ),
        out_specs=(
            P("dp", None, "slab", None, None, None),
            P(("slab", "dp"), None),
            P(("slab", "dp"), None),
            P(("slab", "dp"), None),
        ),
        check_vma=False,
    )
```

profile of v0, /device:TPU:0, one launch (start us, length us, event | category | flops | bytes accessed | tf_op | source)
XLA Modules:
  0.0 458.0 jit_solution(18084580664319161008)
XLA Ops:
  7.2 1.5 convert_bitcast_fusion
  8.8 1.0 broadcast_maximum_fusion
  9.8 0.9 pad_maximum_fusion.32
  10.7 1.3 collective-permute-start.1
  12.0 4.6 collective-permute-start
  17.3 0.8 collective-permute-done.1
  18.1 1.2 collective-permute-done
  19.5 1.2 pad_slice_fusion.74
  20.8 0.9 pad_slice_fusion.1
  21.7 1.0 pad_maximum_fusion.1
  22.7 1.0 pad_maximum_fusion.2
  23.7 1.0 pad_maximum_fusion.5
  24.7 1.1 pad_maximum_fusion.8
  25.8 1.1 pad_maximum_fusion.9
  26.8 1.2 pad_slice_fusion.2
  28.1 1.0 pad_maximum_fusion.20
  29.1 1.0 pad_maximum_fusion.21
  30.1 1.0 pad_maximum_fusion.24
  31.1 1.0 pad_maximum_fusion.27
  32.1 1.0 pad_maximum_fusion.28
  33.1 1.4 pad_maximum_fusion.3
  34.5 1.5 pad_maximum_fusion.6
  36.0 1.4 pad_maximum_fusion.22
  37.4 1.4 pad_maximum_fusion.25
  38.8 172.4 %all-gather.3.cloned.1.call-done = bf16[128,108,128]{2,1,0:T(8,128)(2,1)} async-done(((bf16[1,108,128]{2,1,0:T(8,128)(2,1)}), bf16[128,108,128]{2,1,0:T(8,128)(2,1)}) %all-gather.3.cloned.1.call-update) | async-done | bytes 3538960 | tf_op jit(solution)/shard_map/all_gather | solution.py:143
  211.2 1.6 fusion.90
  213.0 1.4 copy.17
  214.4 1.6 fusion.79
  221.7 1.3 collective-permute-start.3
  223.0 5.2 %collective-permute-start.2 = (bf16[2,2,1,8,16,128]{5,4,3,2,1,0:T(8,128)(2,1)}, bf16[2,2,1,8,16,128]{5,4,3,2,1,0:T(8,128)(2,1)}, u32[]{:S(2)}, u32[]{:S(2)}) collective-permute-start(bf16[2,2,1,8,16,128]{5,4,3,2,1,0:T(8,128)(2,1)} %get-tuple-element.13), channel_id=1, source_target_pairs={{0,4},{4,8},{8,12},{12,16},{16,20},{20,24},{24,28},{28,32},{32,36}... | collective-permute-start | bytes 393224 | tf_op jit(solution)/shard_map/ppermute | solution.py:20
  228.5 1.4 copy.18
  230.4 1.1 pad_maximum_fusion.10
  231.6 1.2 pad_slice_fusion.50
  233.3 1.2 pad_slice_fusion.26
  239.9 4.6 %collective-permute-start.4 = (bf16[2,1,8,16,128]{4,3,2,1,0:T(8,128)(2,1)S(1)}, bf16[2,1,8,16,128]{4,3,2,1,0:T(8,128)(2,1)S(1)}, u32[]{:S(2)}, u32[]{:S(2)}) collective-permute-start(bf16[2,1,8,16,128]{4,3,2,1,0:T(8,128)(2,1)S(1)} %slice.703), channel_id=1, source_target_pairs={{0,4},{4,8},{8,12},{12,16},{16,20},{20,24},{24,28},{28,32},{32,36}... | collective-permute-start | bytes 196616 | tf_op jit(solution)/shard_map/ppermute | solution.py:29
  253.1 2.9 copy-done.2
  260.0 0.8 slice.596
  264.7 0.8 slice.605
  269.3 0.8 slice.614
  270.7 2.4 fusion.91
  273.1 5.2 %copy.20 = f32[27,256,128]{2,1,0:T(8,128)} copy(f32[27,256,128]{1,2,0:T(8,128)} %bitcast.181) | data formatting | bytes 7077888 | tf_op jit(solution)/shard_map/transpose | solution.py:134
  278.2 4.1 constant_dynamic-update-slice_fusion.27
  282.4 1.5 slice-done
  283.9 1.4 reshape.171
  285.3 2.6 copy.19
  287.9 1.0 fusion.9
  289.0 160.7 %all-reduce.7.cloned.1.call-done = f32[13824,128]{1,0:T(8,128)} async-done(((f32[13824,128]{1,0:T(8,128)}), f32[13824,128]{1,0:T(8,128)}) %all-reduce.7.cloned.1.call-update) | async-done | bytes 7077904 | tf_op jit(solution)/shard_map/psum | solution.py:170
  449.7 1.5 divide_subtract_fusion
  (174 shorter events, 33.6 us)
Async XLA Ops:
  7.2 263.5 %copy-start = (bf16[1,2,2,4,8,256]{5,4,3,2,1,0:T(8,128)(2,1)S(1)}, bf16[1,2,2,4,8,256]{5,4,3,2,1,0:T(8,128)(2,1)}, u32[]{:S(2)}) copy-start(bf16[1,2,2,4,8,256]{5,4,3,2,1,0:T(8,128)(2,1)} %param.7) | copy-start | bytes 196612
  7.2 12.1 %copy-start.1 = (bf16[1,2,4,8,16,128]{5,4,3,2,1,0:T(8,128)(2,1)S(1)}, bf16[1,2,4,8,16,128]{5,4,3,2,1,0:T(8,128)(2,1)}, u32[]{:S(2)}) copy-start(bf16[1,2,4,8,16,128]{5,4,3,2,1,0:T(8,128)(2,1)} %param.10) | copy-start | bytes 786436
  7.2 9.4 %copy-start.23 = (bf16[1,2,4,8,16,128]{5,4,3,2,1,0:T(8,128)(2,1)S(1)}, bf16[1,2,4,8,16,128]{5,4,3,2,1,0:T(8,128)(2,1)}, u32[]{:S(2)}) copy-start(bf16[1,2,4,8,16,128]{5,4,3,2,1,0:T(8,128)(2,1)} %param.8) | copy-start | bytes 786436
  7.2 204.0 %all-gather.3.cloned.1.call-start = ((), (), s32[]{:S(2)}) async-start(), calls=%async_computation.1 | async-start | bytes 3698688 | tf_op jit(solution)/shard_map/all_gather | solution.py:143
  8.8 440.9 %all-reduce.7.cloned.1.call-start = ((), (), s32[]{:S(2)}) async-start(), calls=%async_computation | async-start | bytes 14155776 | tf_op jit(solution)/shard_map/psum | solution.py:170
  10.7 7.4 %collective-permute-start.1 = (bf16[2,2,1,8,16,128]{5,4,3,2,1,0:T(8,128)(2,1)S(1)}, bf16[2,2,1,8,16,128]{5,4,3,2,1,0:T(8,128)(2,1)S(1)}, u32[]{:S(2)}, u32[]{:S(2)}) collective-permute-start(bf16[2,2,1,8,16,128]{5,4,3,2,1,0:T(8,128)(2,1)S(1)} %get-tuple-element.16), channel_id=1, source_target_pairs={{4,0},{8,4},{12,8},{16,12},{20,16},{24,20},{28,24},{32,28},{36,32}... | collective-permute-start | bytes 393224 | tf_op jit(solution)/shard_map/ppermute | solution.py:21
  12.0 7.3 %collective-permute-start = (bf16[2,2,1,8,16,128]{5,4,3,2,1,0:T(8,128)(2,1)S(1)}, bf16[2,2,1,8,16,128]{5,4,3,2,1,0:T(8,128)(2,1)S(1)}, u32[]{:S(2)}, u32[]{:S(2)}) collective-permute-start(bf16[2,2,1,8,16,128]{5,4,3,2,1,0:T(8,128)(2,1)S(1)} %get-tuple-element.15), channel_id=1, source_target_pairs={{0,4},{4,8},{8,12},{12,16},{16,20},{20,24},{24,28},{28,32},{32,36}... | collective-permute-start | bytes 393224 | tf_op jit(solution)/shard_map/ppermute | solution.py:20
  214.4 1.6 copy-start.15
  214.4 2.0 copy-start.18
  216.1 1.1 copy-start.16
  216.5 1.2 copy-start.14
  217.2 1.2 copy-start.19
  217.7 1.2 copy-start.17
  218.4 1.2 copy-start.13
  218.9 1.2 copy-start.8
  219.6 1.0 copy-start.20
  220.0 1.0 copy-start.21
  221.7 8.2 %collective-permute-start.3 = (bf16[2,2,1,8,16,128]{5,4,3,2,1,0:T(8,128)(2,1)}, bf16[2,2,1,8,16,128]{5,4,3,2,1,0:T(8,128)(2,1)}, u32[]{:S(2)}, u32[]{:S(2)}) collective-permute-start(bf16[2,2,1,8,16,128]{5,4,3,2,1,0:T(8,128)(2,1)} %get-tuple-element.14), channel_id=1, source_target_pairs={{4,0},{8,4},{12,8},{16,12},{20,16},{24,20},{28,24},{32,28},{36,32}... | collective-permute-start | bytes 393224 | tf_op jit(solution)/shard_map/ppermute | solution.py:21
  223.0 7.4 %collective-permute-start.2 = (bf16[2,2,1,8,16,128]{5,4,3,2,1,0:T(8,128)(2,1)}, bf16[2,2,1,8,16,128]{5,4,3,2,1,0:T(8,128)(2,1)}, u32[]{:S(2)}, u32[]{:S(2)}) collective-permute-start(bf16[2,2,1,8,16,128]{5,4,3,2,1,0:T(8,128)(2,1)} %get-tuple-element.13), channel_id=1, source_target_pairs={{0,4},{4,8},{8,12},{12,16},{16,20},{20,24},{24,28},{28,32},{32,36}... | collective-permute-start | bytes 393224 | tf_op jit(solution)/shard_map/ppermute | solution.py:20
  228.5 1.9 copy-start.22
  238.9 1.0 copy-start.24
  239.9 16.1 %collective-permute-start.4 = (bf16[2,1,8,16,128]{4,3,2,1,0:T(8,128)(2,1)S(1)}, bf16[2,1,8,16,128]{4,3,2,1,0:T(8,128)(2,1)S(1)}, u32[]{:S(2)}, u32[]{:S(2)}) collective-permute-start(bf16[2,1,8,16,128]{4,3,2,1,0:T(8,128)(2,1)S(1)} %slice.703), channel_id=1, source_target_pairs={{0,4},{4,8},{8,12},{12,16},{16,20},{20,24},{24,28},{28,32},{32,36}... | collective-permute-start | bytes 196616 | tf_op jit(solution)/shard_map/ppermute | solution.py:29
  248.0 1.1 copy-start.6
  248.0 1.6 copy-start.7
  248.4 1.6 copy-start.11
  249.1 1.3 copy-start.9
  249.6 1.3 copy-start.5
  250.0 1.4 copy-start.12
  250.5 1.4 copy-start.10
  250.9 1.3 copy-start.3
  251.4 1.3 copy-start.4
  253.1 3.0 copy-start.2
  282.4 1.5 slice-start
  287.9 161.8 %copy-start.25 = (f32[108,128]{1,0:T(8,128)S(1)}, f32[108,128]{1,0:T(8,128)}, u32[]{:S(2)}) copy-start(f32[108,128]{1,0:T(8,128)} %param.11) | copy-start | bytes 165892
  287.9 161.8 %copy-start.26 = (f32[108,128]{1,0:T(8,128)S(1)}, f32[108,128]{1,0:T(8,128)}, u32[]{:S(2)}) copy-start(f32[108,128]{1,0:T(8,128)} %param.12) | copy-start | bytes 165892
  287.9 161.8 %copy-start.27 = (f32[108,128]{1,0:T(8,128)S(1)}, f32[108,128]{1,0:T(8,128)}, u32[]{:S(2)}) copy-start(f32[108,128]{1,0:T(8,128)} %param.13) | copy-start | bytes 165892
Sparse Core Ops, SparseCore 0:
  10.3 200.8 all-gather.2
  282.5 167.1 all-reduce.6
where the time goes:
time: 459 us; the launch traced here: 458 us
  waiting for transfers between devices  336 us (73%)
  local copies, waits for them, and re-layouts  46.5 us (10%)
  other arithmetic  24.8 us (5%)
  matrix products  18.9 us (4%)
  starting transfers between devices  17 us (4%)
  between operations  15.2 us (3%)
    all_gather x1, waiting for transfers between devices, body(): lax.all_gather(master.astype(jnp.bfloat16), ('slab', 'dp'), axis=0, tiled...  172 us
    psum x1, waiting for transfers between devices, body(): totals = lax.psum(partial_value, ('slab', 'dp'))  161 us
    slice x27, local copies, waits for them, and re-layouts, upconv_back(): lateral[:, depth_tap:depth_tap + 2 * coarse_depth:2, row_tap:row_tap + 2...  13.7 us
    ppermute x2, starting transfers between devices, padded_2(): before = lax.ppermute(last, axis, up)  9.75 us
  transfers between devices with their start and end apart: 7, of which 5 were waited for; matrix products, arithmetic and copies ran while one was open for 8% of the time, Pallas kernels for 0%

commit v1 on v0

v1 whole, which is shorter than its diff:
```python
import jax
import jax.numpy as jnp
from jax import lax
from jax.experimental import pallas as pl
from jax.experimental.pallas import tpu as pltpu
from jax.sharding import PartitionSpec as P

beta_one = 0.9
beta_two = 0.999
adam_step = 10.0
learn_rate = 0.01
adam_eps = 1e-08

F32 = jnp.float32
BF16 = jnp.bfloat16
MESH = pl.DeviceIdType.MESH

ROWS = 108
TOTAL = 13824
FILTER = 3456
START = (0, 48, 80)
HOLD = (48, 32, 32)
VALID = (48, 32, 28)
ORDER = (("y", "z", "x"), ("z", "x", "y"), ("x", "y", "z"))


def nt(left, right):
    return lax.dot_general(
        left, right, (((1,), (1,)), ((), ())), preferred_element_type=F32
    )


def nn(left, right):
    return jnp.dot(left, right, preferred_element_type=F32)


def kernel(
    master, grad_out, pre_mid, pre_up, coarse,
    coarse_grad, summed,
    g0, g1, g2, sb0, sb1, sb2, rb0, rb1, rb2, t0, t1, t2, ra0, ra1, ra2,
    u0, u1, u2, rc0, rc1, rc2, v0, v1, v2, rd0, rd1, rd2,
    wflat, fflat, w_one, w_two, w_up, x_out, x_mid, act_t, mid_raw, up_raw, gathered, halo_out, halo_mid,
    ag_send, ag_recv, core_send, core_recv, rs_send, rs_recv, swap_send, swap_recv,
    halo_send, halo_recv,
):
    gat, sbs, rbs, tot = (g0, g1, g2), (sb0, sb1, sb2), (rb0, rb1, rb2), (t0, t1, t2)
    ras, us, rcs, vs, rds = (
        (ra0, ra1, ra2), (u0, u1, u2), (rc0, rc1, rc2), (v0, v1, v2), (rd0, rd1, rd2),
    )
    slab, dp = lax.axis_index("slab"), lax.axis_index("dp")
    at = {
        "x": lax.rem(slab // 4, 4),
        "y": (slab // 16) * 2 + dp // 2,
        "z": lax.rem(slab, 4),
    }
    core = lax.rem(dp, 2)
    other = 1 - core

    def device(where, which):
        return (
            (where["y"] // 2) * 16 + where["x"] * 4 + where["z"],
            lax.rem(where["y"], 2) * 2 + which,
        )

    def ahead(axis, step):
        moved = dict(at)
        moved[axis] = lax.rem(at[axis] + step, 4)
        return device(moved, core)

    def back(axis, step):
        return lax.rem(at[axis] + 4 - step, 4)

    partner = device(at, other)
    after = (lax.rem(slab + 1, 32), dp)
    before = (lax.rem(slab + 31, 32), dp)

    def copy(src, dst, send, recv, target):
        return pltpu.make_async_remote_copy(
            src_ref=src, dst_ref=dst, send_sem=send, recv_sem=recv,
            device_id=target, device_id_type=MESH,
        )

    barrier = pltpu.get_barrier_semaphore()
    targets = [partner, after, before]
    targets += [ahead(axis, step) for axis in ("x", "y", "z") for step in (1, 2, 3)]
    for target in targets:
        pl.semaphore_signal(barrier, inc=1, device_id=target, device_id_type=MESH)

    for part in range(3):
        axes = ORDER[part]
        rows = master[START[part] : START[part] + VALID[part], :]
        if HOLD[part] > VALID[part]:
            rows = jnp.concatenate(
                [rows, jnp.zeros((HOLD[part] - VALID[part], 128), F32)], axis=0
            )
        gat[part][core, at[axes[2]], at[axes[1]], at[axes[0]]] = rows.astype(BF16)
    pl.semaphore_wait(barrier, len(targets))

    started = []

    def go(c):
        c.start()
        started.append(c)
        return c

    halo_up = go(copy(grad_out.at[:, 3], halo_out.at[0], halo_send.at[0], halo_recv.at[0], after))
    halo_down = go(copy(grad_out.at[:, 0], halo_out.at[1], halo_send.at[1], halo_recv.at[1], before))

    def piece(part, which, level, coords):
        axes = ORDER[part]
        place = [coords[axes[2]], coords[axes[1]], coords[axes[0]]][: 3 - level]
        return gat[part].at[tuple([which] + place)]

    def gather_copy(part, level, step):
        src = piece(part, core, level, at)
        sem = (part, level, step - 1)
        return copy(src, src, ag_send.at[sem], ag_recv.at[sem], ahead(ORDER[part][level], step))

    def arrived(part, level, step, which):
        moved = dict(at)
        moved[ORDER[part][level]] = back(ORDER[part][level], step)
        return piece(part, which, level, moved)

    def gather_start(level):
        for step in (1, 3, 2):
            for part in range(3):
                go(gather_copy(part, level, step))

    def core_copy(part, number, ref):
        return copy(ref, ref, core_send.at[part, number], core_recv.at[part, number], partner)

    def gather_wait(level, passed):
        for step in (1, 3, 2):
            for part in range(3):
                ref = arrived(part, level, step, core)
                sem = (part, level, step - 1)
                copy(ref, ref, ag_send.at[sem], ag_recv.at[sem], partner).wait_recv()
                if passed:
                    go(core_copy(part, (level - 1) * 3 + step, ref))

    gather_start(0)

    row = lax.broadcasted_iota(jnp.int32, (128, 128), 0)
    lane = lax.broadcasted_iota(jnp.int32, (128, 128), 1)
    breadth = lax.rem(row, 16)
    for ext in (x_out, x_mid):
        ext[:, :, 0] = jnp.zeros((2, 6, 16, 384), BF16)
        ext[:, :, 9] = jnp.zeros((2, 6, 16, 384), BF16)
    fflat[TOTAL : TOTAL + 8, :] = jnp.zeros((8, 128), F32)

    def widen(ext, sample, layer, value):
        later = jnp.where(breadth == 15, 0.0, pltpu.roll(value, 127, 0))
        earlier = jnp.where(breadth == 0, 0.0, pltpu.roll(value, 1, 0))
        wide = jnp.concatenate(
            [later.astype(BF16), value.astype(BF16), earlier.astype(BF16)], axis=1
        )
        ext[sample, layer, 1:9] = wide.reshape(8, 16, 384)

    def transposed_act(pre):
        for sample in range(2):
            for layer in range(4):
                value = jnp.maximum(pre[sample, layer].reshape(128, 128).astype(F32), 0.0)
                turned = value.T
                first = sample * 4 + layer
                columns = slice(first * 128, first * 128 + 128)
                low = jnp.where(lane < 16, 0.0, pltpu.roll(turned, 16, 1))
                high = jnp.where(lane >= 112, 0.0, pltpu.roll(turned, 112, 1))
                act_t[0:128, columns] = low.astype(BF16)
                act_t[128:256, columns] = turned.astype(BF16)
                act_t[256:384, columns] = high.astype(BF16)

    def own_layers(index, carry):
        sample, layer = index // 4, lax.rem(index, 4)
        widen(x_out, sample, layer + 1, grad_out[sample, layer].reshape(128, 128).astype(F32))
        return carry

    def edges(ext, halo):
        for sample in range(2):
            low = halo[0, sample].reshape(128, 128).astype(F32)
            widen(ext, sample, 0, jnp.where(slab > 0, low, 0.0))
            high = halo[1, sample].reshape(128, 128).astype(F32)
            widen(ext, sample, 5, jnp.where(slab < 31, high, 0.0))

    def filter_grad(ext, first, depth):
        right = ext[:, 2 - depth : 6 - depth, 1:9].reshape(1024, 384)
        out = nn(act_t[...], right)
        for height in range(3):
            for col in range(3):
                start = first + ((depth * 3 + height) * 3 + col) * 128
                fflat[start : start + 128, :] = out[
                    height * 128 : height * 128 + 128, col * 128 : col * 128 + 128
                ]

    def back_conv(ext, weight, layer):
        acc = jnp.zeros((256, 128), F32)
        for depth in range(3):
            for height in range(3):
                left = ext[:, layer + 2 - depth, 2 - height : 10 - height].reshape(256, 384)
                acc = acc + nt(left, weight[depth * 3 + height])
        return acc

    transposed_act(pre_mid)
    lax.fori_loop(0, 8, own_layers, 0)
    gather_wait(0, False)
    gather_start(1)
    for part in range(3):
        go(core_copy(part, 0, piece(part, core, 1, at)))
    halo_up.wait_recv()
    halo_down.wait_recv()
    edges(x_out, halo_out)
    filter_grad(x_out, FILTER, 1)
    gather_wait(1, True)
    gather_start(2)
    filter_grad(x_out, FILTER, 0)
    filter_grad(x_out, FILTER, 2)
    gather_wait(2, True)
    for part in range(3):
        for number in range(7):
            if number == 0:
                ref = piece(part, other, 1, at)
            else:
                ref = arrived(part, 1 + (number - 1) // 3, (number - 1) % 3 + 1, other)
            core_copy(part, number, ref).wait_recv()

    def place(chip, which):
        where = {"x": lax.rem(chip // 8, 4), "y": (chip // 32) * 2 + lax.rem(chip, 2), "z": lax.rem(chip // 2, 4)}
        return where

    def unpack(chip, carry):
        where = place(chip, 0)
        base = pl.multiple_of(chip * 216, 8)
        pieces = []
        for which in range(2):
            for part in range(3):
                axes = ORDER[part]
                value = gat[part][which, where[axes[2]], where[axes[1]], where[axes[0]]]
                pieces.append(value.astype(F32)[: VALID[part]])
        wflat[pl.ds(base, 216), :] = jnp.concatenate(pieces, axis=0)
        return carry

    lax.fori_loop(0, 64, unpack, 0)

    def taps(index, carry):
        for col in range(3):
            columns = slice(col * 128, col * 128 + 128)
            start = pl.multiple_of((index * 3 + col) * 128, 128)
            w_one[index, :, columns] = wflat[pl.ds(start, 128), :].astype(BF16)
            w_two[index, :, columns] = wflat[pl.ds(start + FILTER, 128), :].astype(BF16)
            start = pl.multiple_of((index * 3 + col) * 256, 128)
            w_up[index, :, columns] = wflat[pl.ds(start + 2 * FILTER, 256), :].astype(BF16)
        return carry

    lax.fori_loop(0, 9, taps, 0)

    def mid_layer(index, carry):
        layer = lax.rem(index + 3, 4)
        value = back_conv(x_out, w_two, layer)
        keep = pre_mid[:, layer].reshape(256, 128).astype(F32) > 0.0
        value = jnp.where(keep, value, 0.0).astype(BF16)
        mid_raw[:, layer] = value.reshape(2, 8, 16, 128)
        for sample in range(2):
            widen(x_mid, sample, layer + 1, value[sample * 128 : sample * 128 + 128].astype(F32))
        return carry

    lax.fori_loop(0, 2, mid_layer, 0)
    mid_up = go(copy(mid_raw.at[:, 3], halo_mid.at[0], halo_send.at[2], halo_recv.at[2], after))
    mid_down = go(copy(mid_raw.at[:, 0], halo_mid.at[1], halo_send.at[3], halo_recv.at[3], before))
    lax.fori_loop(2, 4, mid_layer, 0)
    transposed_act(pre_up)
    filter_grad(x_mid, 0, 1)
    mid_up.wait_recv()
    mid_down.wait_recv()
    edges(x_mid, halo_mid)

    def up_layer(index, carry):
        layer = lax.rem(index + 3, 4)
        value = back_conv(x_mid, w_one, layer)
        keep = pre_up[:, layer].reshape(256, 128).astype(F32) > 0.0
        value = jnp.where(keep, value, 0.0).astype(BF16)
        up_raw[:, layer + 1] = value.reshape(2, 128, 128)
        return carry

    lax.fori_loop(0, 1, up_layer, 0)
    up_next = go(copy(up_raw.at[:, 4], up_raw.at[:, 0], halo_send.at[4], halo_recv.at[4], after))
    lax.fori_loop(1, 4, up_layer, 0)
    filter_grad(x_mid, 0, 0)
    filter_grad(x_mid, 0, 2)
    up_next.wait_recv()

    pick_row = lax.broadcasted_iota(jnp.int32, (288, 128), 0)
    pick_lane = lax.broadcasted_iota(jnp.int32, (288, 128), 1)
    tap, coarse_row, coarse_col = pick_row // 32, lax.rem(pick_row // 8, 4), lax.rem(pick_row, 8)
    fine_row = 2 * coarse_row + tap // 3 - 1
    fine_col = 2 * coarse_col + lax.rem(tap, 3) - 1
    chosen = (fine_row >= 0) & (fine_col >= 0) & (pick_lane == fine_row * 16 + fine_col)
    pick = jnp.where(chosen, 1.0, 0.0).astype(BF16)
    for sample in range(2):
        for layer in range(5):
            value = up_raw[sample, layer]
            if layer == 0:
                value = jnp.where(slab > 0, value.astype(F32), 0.0).astype(BF16)
            picked = nn(pick, value).astype(BF16)
            for depth, quarter in ((layer, 0), (layer - 2, 1)):
                if 0 <= depth < 3:
                    first = (sample * 2 + quarter) * 32
                    for tap in range(9):
                        column = (depth * 9 + tap) * 128
                        gathered[first : first + 32, column : column + 128] = picked[
                            tap * 32 : tap * 32 + 32
                        ]
    acc = jnp.zeros((128, 256), F32)
    coarse_t = coarse[...].reshape(128, 256).astype(F32).T.astype(BF16)
    for index in range(9):
        column = index * 384
        block = gathered[:, column : column + 384]
        acc = acc + nt(block, w_up[index])
        out = nn(coarse_t, block)
        for col in range(3):
            start = 2 * FILTER + (index * 3 + col) * 256
            fflat[start : start + 256, :] = out[:, col * 128 : col * 128 + 128]
    coarse_grad[...] = acc.astype(BF16)

    def pack(chip, carry):
        where = place(chip, 0)
        base = pl.multiple_of(chip * 216, 8)
        value = fflat[pl.ds(base, 224), :]
        for which in range(2):
            for part in range(3):
                axes = ORDER[part]
                start = which * ROWS + START[part]
                rows = value[start : start + HOLD[part]].astype(BF16)
                sbs[part][which, where[axes[2]], where[axes[1]], where[axes[0]]] = rows
        return carry

    lax.fori_loop(0, 64, pack, 0)
    swaps = [
        go(copy(sbs[part].at[other], rbs[part], swap_send.at[part], swap_recv.at[part], partner))
        for part in range(3)
    ]

    def scatter(part, level, src, dst):
        axis = ORDER[part][2 - level]
        out = []
        for step in (1, 3, 2):
            sem = (part, level, step - 1)
            out.append(
                go(
                    copy(
                        src.at[lax.rem(at[axis] + step, 4)], dst.at[step - 1],
                        rs_send.at[sem], rs_recv.at[sem], ahead(axis, step),
                    )
                )
            )
        return out

    first = []
    for part in range(3):
        swaps[part].wait_recv()

        def add(index, carry, part=part):
            total = sbs[part][core, index // 4, lax.rem(index, 4)].astype(F32)
            total = total + rbs[part][index // 4, lax.rem(index, 4)].astype(F32)
            tot[part][index // 4, lax.rem(index, 4)] = total.astype(BF16)
            return carry

        lax.fori_loop(0, 16, add, 0)
        first.append(scatter(part, 0, tot[part], ras[part]))
    second = []
    for part in range(3):
        for c in first[part]:
            c.wait_recv()
        mine = at[ORDER[part][2]]

        def add(index, carry, part=part, mine=mine):
            total = tot[part][mine, index].astype(F32)
            for step in range(3):
                total = total + ras[part][step, index].astype(F32)
            us[part][index] = total.astype(BF16)
            return carry

        lax.fori_loop(0, 4, add, 0)
        second.append(scatter(part, 1, us[part], rcs[part]))
    third = []
    for part in range(3):
        for c in second[part]:
            c.wait_recv()
        total = us[part][at[ORDER[part][1]]].astype(F32)
        for step in range(3):
            total = total + rcs[part][step].astype(F32)
        vs[part][...] = total.astype(BF16)
        third.append(scatter(part, 2, vs[part], rds[part]))
    for part in range(3):
        for c in third[part]:
            c.wait_recv()
        total = vs[part][at[ORDER[part][0]]].astype(F32)
        for step in range(3):
            total = total + rds[part][step].astype(F32)
        summed[START[part] : START[part] + VALID[part], :] = total[: VALID[part]]
    for c in started:
        c.wait_send()


def body(coarse_in, pre_up, pre_mid, grad_out, master, moment, second):
    vmem = pl.BlockSpec(memory_space=pltpu.VMEM)
    scratch = []
    for shape in ((2, 4, 4, 4), (2, 4, 4, 4), (4, 4, 4), (4, 4, 4), (3, 4, 4), (4, 4), (3, 4), (4,), (3,)):
        scratch += [pltpu.VMEM(shape + (hold, 128), BF16) for hold in HOLD]
    scratch += [
        pltpu.VMEM((TOTAL, 128), F32),
        pltpu.VMEM((TOTAL + 8, 128), F32),
        pltpu.VMEM((9, 128, 384), BF16),
        pltpu.VMEM((9, 128, 384), BF16),
        pltpu.VMEM((9, 256, 384), BF16),
        pltpu.VMEM((2, 6, 10, 16, 384), BF16),
        pltpu.VMEM((2, 6, 10, 16, 384), BF16),
        pltpu.VMEM((384, 1024), BF16),
        pltpu.VMEM((2, 4, 8, 16, 128), BF16),
        pltpu.VMEM((2, 5, 128, 128), BF16),
        pltpu.VMEM((128, FILTER), BF16),
        pltpu.VMEM((2, 2, 8, 16, 128), BF16),
        pltpu.VMEM((2, 2, 8, 16, 128), BF16),
    ]
    for shape in ((3, 3, 3), (3, 7), (3, 3, 3), (3,), (5,)):
        scratch += [pltpu.SemaphoreType.DMA(shape)] * 2
    coarse_grad, summed = pl.pallas_call(
        kernel,
        out_shape=(
            jax.ShapeDtypeStruct((128, 256), BF16),
            jax.ShapeDtypeStruct((ROWS, 128), F32),
        ),
        in_specs=[vmem] * 5,
        out_specs=(vmem, vmem),
        scratch_shapes=scratch,
        compiler_params=pltpu.CompilerParams(
            collective_id=0, has_side_effects=True, vmem_limit_bytes=56 * 1024 * 1024
        ),
    )(
        master,
        grad_out.reshape(grad_out.shape[1:]),
        pre_mid.reshape(pre_mid.shape[1:]),
        pre_up.reshape(pre_up.shape[1:]),
        coarse_in.reshape(128, 256),
    )
    mean_grad = summed / 8.0
    new_moment = beta_one * moment + (1.0 - beta_one) * mean_grad
    new_second = beta_two * second + (1.0 - beta_two) * mean_grad * mean_grad
    corrected = new_moment / (1.0 - beta_one**adam_step)
    scaled = jnp.sqrt(new_second / (1.0 - beta_two**adam_step)) + adam_eps
    new_master = master - learn_rate * corrected / scaled
    return (coarse_grad.reshape(coarse_in.shape), new_master, new_moment, new_second)


def solution(mesh):
    wide = P("dp", None, "slab", None, None, None)
    flat = P(("slab", "dp"), None)
    return jax.shard_map(
        body,
        mesh=mesh,
        in_specs=(wide, wide, wide, wide, flat, flat, flat),
        out_specs=(wide, flat, flat, flat),
        check_vma=False,
    )
```

time: 459 us -> 74.3 us (0.16)
  waiting for transfers between devices: 336 us -> 0 us
  Pallas kernels: 0 us -> 71.3 us
  local copies, waits for them, and re-layouts: 46.5 us -> 0.65 us
  other arithmetic: 24.8 us -> 1.53 us
  matrix products: 18.9 us -> 0 us
  starting transfers between devices: 17 us -> 0 us
  between operations: 15.2 us -> 0.7 us
    all_gather x1 -> x0, waiting for transfers between devices: 172 us -> none  [body(): lax.all_gather(master.astype(jnp.bfloat16), ('slab', 'dp'), axis=0, tiled...]
    psum x1 -> x0, waiting for transfers between devices: 161 us -> none  [body(): totals = lax.psum(partial_value, ('slab', 'dp'))]
    pallas_call x0 -> x1, Pallas kernels: none -> 71.3 us  [body(): pl.pallas_call(kernel, out_shape=(jax.ShapeDtypeStruct((128, 256), BF16),...]
    slice x38 -> x0, local copies, waits for them, and re-layouts: 23.4 us -> none  [the longest x27 13.7 us: upconv_back(): lateral[:, depth_tap:depth_tap + 2 * coarse_depth:2, row_tap:row_tap + 2...]
    dot_general x38 -> x0, matrix products: 18.9 us -> none  [the longest x18 7.82 us: correlate(): jnp.dot(columns.reshape(-1, 3 * in_width), weight[row_start:row_start + 3...]
    concatenate x26 -> x0, other arithmetic: 18.2 us -> none  [the longest x16 9.04 us: correlate(): jnp.concatenate([lateral[:, depth_tap:depth_tap + inner_depth, row_tap:ro...]
    ppermute x5 -> x0, starting transfers between devices: 16.9 us -> none  [the longest x2 9.75 us: padded_2(): before = lax.ppermute(last, axis, up)]
    transpose x6 -> x0, local copies, waits for them, and re-layouts: 10.7 us -> none  [the longest x1 5.17 us: upconv_back(): filter_part = filter_part.reshape(coarse_width, 27, fine_width).transpose...]
  transfers between devices with their start and end apart: 7 -> 0, of which waited for: 5 -> 0; matrix products, arithmetic and copies ran while one was open for 8% -> 0% of each run, Pallas kernels for 0% -> 0%
where the time goes in v1:
time: 74.3 us; the launch traced here: 74.1 us
  Pallas kernels  71.3 us (96%)
  other arithmetic  1.53 us (2%)
    pallas_call x1, Pallas kernels, body(): pl.pallas_call(kernel, out_shape=(jax.ShapeDtypeStruct((128, 256), BF16),...  71.3 us
    sub x1, other arithmetic, body(): new_master = master - learn_rate * corrected / scaled  1.53 us

profile of v1, /device:TPU:0, one launch (start us, length us, event | category | flops | bytes accessed | tf_op | source)
XLA Modules:
  0.0 74.1 jit_solution(4873039226269424448)
XLA Ops:
  0.6 0.0 copy-start
  0.6 0.0 copy-start.2
  0.7 0.0 copy-start.3
  0.7 71.3 %shard_map.102 = (bf16[128,256]{1,0:T(8,128)(2,1)}, f32[108,128]{1,0:T(8,128)}) custom-call(f32[108,128]{1,0:T(8,128)} %master.1, bf16[2,4,8,16,128]{4,3,2,1,0:T(8,128)(2,1)} %bitcast.5, bf16[2,4,8,16,128]{4,3,2,1,0:T(8,128)(2,1)} %bitcast.6, bf16[2,4,8,16,128]{4,3,2,1,0:T(8,128)(2,1)} %bitcast.7, bf16[128,256]{1,0:T(8,128)(2,1)} %bitcast.8), custom_call_target="tpu_custom_call" | custom-call | tf_op jit(solution)/shard_map/pallas_call | solution.py:425
  71.9 0.0 copy-done
  71.9 0.0 copy-done.2
  71.9 0.0 copy-done.3
  72.0 0.0 copy-start.1
  72.0 1.5 %divide_subtract_fusion = (f32[108,128]{1,0:T(8,128)}, f32[108,128]{1,0:T(8,128)}, f32[108,128]{1,0:T(8,128)}) fusion(f32[108,128]{1,0:T(8,128)S(1)} %copy-done, f32[108,128]{1,0:T(8,128)} %get-tuple-element.7, f32[108,128]{1,0:T(8,128)S(1)} %copy-done.2, f32[108,128]{1,0:T(8,128)S(1)} %copy-done.3), kind=kLoop, calls=%fused_computation | loop fusion | flops 179712 | bytes 387072 | tf_op jit(solution)/shard_map/sub | solution.py:449
  73.5 0.0 copy-done.1
  73.5 0.6 copy.12
Async XLA Ops:
  0.6 71.3 %copy-start = (f32[108,128]{1,0:T(8,128)S(1)}, f32[108,128]{1,0:T(8,128)}, u32[]{:S(2)}) copy-start(f32[108,128]{1,0:T(8,128)} %master.1) | copy-start | bytes 165892
  0.6 71.3 %copy-start.2 = (f32[108,128]{1,0:T(8,128)S(1)}, f32[108,128]{1,0:T(8,128)}, u32[]{:S(2)}) copy-start(f32[108,128]{1,0:T(8,128)} %param.12) | copy-start | bytes 165892
  0.7 71.3 %copy-start.3 = (f32[108,128]{1,0:T(8,128)S(1)}, f32[108,128]{1,0:T(8,128)}, u32[]{:S(2)}) copy-start(f32[108,128]{1,0:T(8,128)} %param.13) | copy-start | bytes 165892
  72.0 1.5 %copy-start.1 = (bf16[128,256]{1,0:T(8,128)(2,1)S(1)}, bf16[128,256]{1,0:T(8,128)(2,1)}, u32[]{:S(2)}) copy-start(bf16[128,256]{1,0:T(8,128)(2,1)} %get-tuple-element.6) | copy-start | bytes 196612

commit v2 on v1

--- a/solution.py
+++ b/solution.py
@@ -21,7 +21,8 @@
 START = (0, 48, 80)
 HOLD = (48, 32, 32)
 VALID = (48, 32, 28)
-ORDER = (("y", "z", "x"), ("z", "x", "y"), ("x", "y", "z"))
+ORDER = (("y", "z", "x"), ("y", "x", "z"), ("z", "x", "y"))
+EARLY, LATE = 0, 1
 
 
 def nt(left, right):
@@ -62,13 +63,13 @@
             lax.rem(where["y"], 2) * 2 + which,
         )
 
+    def moved(axis, step):
+        where = dict(at)
+        where[axis] = lax.rem(at[axis] + step, 4)
+        return where
+
     def ahead(axis, step):
-        moved = dict(at)
-        moved[axis] = lax.rem(at[axis] + step, 4)
-        return device(moved, core)
-
-    def back(axis, step):
-        return lax.rem(at[axis] + 4 - step, 4)
+        return device(moved(axis, step), core)
 
     partner = device(at, other)
     after = (lax.rem(slab + 1, 32), dp)
@@ -86,14 +87,21 @@
     for target in targets:
         pl.semaphore_signal(barrier, inc=1, device_id=target, device_id_type=MESH)
 
+    def block(ref, part, lead, where):
+        axes = ORDER[part]
+        if part == 2:
+            inner = [lax.rem(where["y"], 2), where["x"], where["z"]]
+        else:
+            inner = [where[axes[2]], where[axes[1]], lax.rem(where["y"], 2)]
+        return tuple([where["y"] // 2] + lead + inner)
+
     for part in range(3):
-        axes = ORDER[part]
         rows = master[START[part] : START[part] + VALID[part], :]
         if HOLD[part] > VALID[part]:
             rows = jnp.concatenate(
                 [rows, jnp.zeros((HOLD[part] - VALID[part], 128), F32)], axis=0
             )
-        gat[part][core, at[axes[2]], at[axes[1]], at[axes[0]]] = rows.astype(BF16)
+        gat[part][block(gat[part], part, [core], at)] = rows.astype(BF16)
     pl.semaphore_wait(barrier, len(targets))
 
     started = []
@@ -103,42 +111,38 @@
         started.append(c)
         return c
 
+    def piece(part, which, level, half, where):
+        place = block(gat[part], part, [which], where)
+        if part == 2:
+            return gat[part].at[place[: 5 - level]]
+        if level == 0:
+            return gat[part].at[place]
+        return gat[part].at[(half,) + place[1 : 5 - level]]
+
+    def gather(part, level, half):
+        axis = ORDER[part][level]
+        out = []
+        for step in (1, 3, 2):
+            sem = (part, level, step - 1, half)
+            src = piece(part, core, level, half, at)
+            go(copy(src, src, ag_send.at[sem], ag_recv.at[sem], ahead(axis, step)))
+            dst = piece(part, core, level, half, moved(axis, 4 - step))
+            out.append(copy(dst, dst, ag_send.at[sem], ag_recv.at[sem], partner))
+        return out
+
+    def core_copy(part, half, number, which):
+        axis = ORDER[part][2]
+        ref = piece(part, which, 2, half, moved(axis, 4 - number))
+        sem = (part, half, number)
+        return copy(ref, ref, core_send.at[sem], core_recv.at[sem], partner)
+
+    def wait_for(copies):
+        for c in copies:
+            c.wait_recv()
+
+    leg = [gather(part, 0, EARLY) for part in range(3)]
     halo_up = go(copy(grad_out.at[:, 3], halo_out.at[0], halo_send.at[0], halo_recv.at[0], after))
     halo_down = go(copy(grad_out.at[:, 0], halo_out.at[1], halo_send.at[1], halo_recv.at[1], before))
-
-    def piece(part, which, level, coords):
-        axes = ORDER[part]
-        place = [coords[axes[2]], coords[axes[1]], coords[axes[0]]][: 3 - level]
-        return gat[part].at[tuple([which] + place)]
-
-    def gather_copy(part, level, step):
-        src = piece(part, core, level, at)
-        sem = (part, level, step - 1)
-        return copy(src, src, ag_send.at[sem], ag_recv.at[sem], ahead(ORDER[part][level], step))
-
-    def arrived(part, level, step, which):
-        moved = dict(at)
-        moved[ORDER[part][level]] = back(ORDER[part][level], step)
-        return piece(part, which, level, moved)
-
-    def gather_start(level):
-        for step in (1, 3, 2):
-            for part in range(3):
-                go(gather_copy(part, level, step))
-
-    def core_copy(part, number, ref):
-        return copy(ref, ref, core_send.at[part, number], core_recv.at[part, number], partner)
-
-    def gather_wait(level, passed):
-        for step in (1, 3, 2):
-            for part in range(3):
-                ref = arrived(part, level, step, core)
-                sem = (part, level, step - 1)
-                copy(ref, ref, ag_send.at[sem], ag_recv.at[sem], partner).wait_recv()
-                if passed:
-                    go(core_copy(part, (level - 1) * 3 + step, ref))
-
-    gather_start(0)
 
     row = lax.broadcasted_iota(jnp.int32, (128, 128), 0)
     lane = lax.broadcasted_iota(jnp.int32, (128, 128), 1)
@@ -199,58 +203,76 @@
                 acc = acc + nt(left, weight[depth * 3 + height])
         return acc
 
-    transposed_act(pre_mid)
-    lax.fori_loop(0, 8, own_layers, 0)
-    gather_wait(0, False)
-    gather_start(1)
-    for part in range(3):
-        go(core_copy(part, 0, piece(part, core, 1, at)))
-    halo_up.wait_recv()
-    halo_down.wait_recv()
-    edges(x_out, halo_out)
-    filter_grad(x_out, FILTER, 1)
-    gather_wait(1, True)
-    gather_start(2)
-    filter_grad(x_out, FILTER, 0)
-    filter_grad(x_out, FILTER, 2)
-    gather_wait(2, True)
-    for part in range(3):
-        for number in range(7):
-            if number == 0:
-                ref = piece(part, other, 1, at)
-            else:
-                ref = arrived(part, 1 + (number - 1) // 3, (number - 1) % 3 + 1, other)
-            core_copy(part, number, ref).wait_recv()
-
-    def place(chip, which):
-        where = {"x": lax.rem(chip // 8, 4), "y": (chip // 32) * 2 + lax.rem(chip, 2), "z": lax.rem(chip // 2, 4)}
-        return where
+    def place(chip):
+        return {"x": lax.rem(chip // 8, 4), "y": (chip // 32) * 2 + lax.rem(chip, 2), "z": lax.rem(chip // 2, 4)}
 
     def unpack(chip, carry):
-        where = place(chip, 0)
+        where = place(chip)
         base = pl.multiple_of(chip * 216, 8)
         pieces = []
         for which in range(2):
             for part in range(3):
-                axes = ORDER[part]
-                value = gat[part][which, where[axes[2]], where[axes[1]], where[axes[0]]]
+                value = gat[part][block(gat[part], part, [which], where)]
                 pieces.append(value.astype(F32)[: VALID[part]])
         wflat[pl.ds(base, 216), :] = jnp.concatenate(pieces, axis=0)
         return carry
 
-    lax.fori_loop(0, 64, unpack, 0)
-
-    def taps(index, carry):
-        for col in range(3):
-            columns = slice(col * 128, col * 128 + 128)
-            start = pl.multiple_of((index * 3 + col) * 128, 128)
-            w_one[index, :, columns] = wflat[pl.ds(start, 128), :].astype(BF16)
-            w_two[index, :, columns] = wflat[pl.ds(start + FILTER, 128), :].astype(BF16)
-            start = pl.multiple_of((index * 3 + col) * 256, 128)
-            w_up[index, :, columns] = wflat[pl.ds(start + 2 * FILTER, 256), :].astype(BF16)
+    def taps(weight, first, width):
+        def one(index, carry):
+            for col in range(3):
+                start = pl.multiple_of((index * 3 + col) * width + first, 128)
+                weight[index, :, col * 128 : col * 128 + 128] = wflat[pl.ds(start, width), :].astype(BF16)
+            return carry
+
+        lax.fori_loop(0, 9, one, 0)
+
+    def pack(chip, carry):
+        where = place(chip)
+        base = pl.multiple_of(chip * 216, 8)
+        value = fflat[pl.ds(base, 224), :]
+        for which in range(2):
+            for part in range(3):
+                start = which * ROWS + START[part]
+                rows = value[start : start + HOLD[part]].astype(BF16)
+                sbs[part][block(sbs[part], part, [which], where)] = rows
         return carry
 
-    lax.fori_loop(0, 9, taps, 0)
+    transposed_act(pre_mid)
+    for part in range(3):
+        wait_for(leg[part])
+    leg = [gather(part, 1, EARLY) for part in range(3)]
+    later_leg = [gather(part, 1, LATE) for part in range(2)]
+    lax.fori_loop(0, 8, own_layers, 0)
+    filter_grad(x_out, FILTER, 1)
+    third = []
+    for part in range(3):
+        wait_for(leg[part])
+        third.append(gather(part, 2, EARLY))
+        go(core_copy(part, EARLY, 0, core))
+    halo_up.wait_recv()
+    halo_down.wait_recv()
+    edges(x_out, halo_out)
+    filter_grad(x_out, FILTER, 0)
+    filter_grad(x_out, FILTER, 2)
+    lax.fori_loop(16, 32, pack, 0)
+
+    def forward(part, half, copies):
+        for step, c in zip((1, 3, 2), copies):
+            c.wait_recv()
+            go(core_copy(part, half, step, core))
+
+    for part in range(3):
+        forward(part, EARLY, third[part])
+    late_third = []
+    for part in range(2):
+        wait_for(later_leg[part])
+        late_third.append(gather(part, 2, LATE))
+        go(core_copy(part, LATE, 0, core))
+    for part in range(3):
+        wait_for([core_copy(part, EARLY, number, other) for number in range(4)])
+
+    lax.fori_loop(16, 32, unpack, 0)
+    taps(w_two, FILTER, 128)
 
     def mid_layer(index, carry):
         layer = lax.rem(index + 3, 4)
@@ -266,8 +288,12 @@
     mid_up = go(copy(mid_raw.at[:, 3], halo_mid.at[0], halo_send.at[2], halo_recv.at[2], after))
     mid_down = go(copy(mid_raw.at[:, 0], halo_mid.at[1], halo_send.at[3], halo_recv.at[3], before))
     lax.fori_loop(2, 4, mid_layer, 0)
+    lax.fori_loop(0, 16, unpack, 0)
+    taps(w_one, 0, 128)
     transposed_act(pre_up)
     filter_grad(x_mid, 0, 1)
+    for part in range(2):
+        forward(part, LATE, late_third[part])
     mid_up.wait_recv()
     mid_down.wait_recv()
     edges(x_mid, halo_mid)
@@ -282,9 +308,92 @@
 
     lax.fori_loop(0, 1, up_layer, 0)
     up_next = go(copy(up_raw.at[:, 4], up_raw.at[:, 0], halo_send.at[4], halo_recv.at[4], after))
-    lax.fori_loop(1, 4, up_layer, 0)
     filter_grad(x_mid, 0, 0)
     filter_grad(x_mid, 0, 2)
+    lax.fori_loop(0, 16, pack, 0)
+
+    def swap(half):
+        return [
+            go(
+                copy(
+                    sbs[part].at[half, other], rbs[part].at[half],
+                    swap_send.at[part, half], swap_recv.at[part, half], partner,
+                )
+            )
+            for part in range(3)
+        ]
+
+    def scatter(part, level, src, dst, sems):
+        axis = ORDER[part][2 - level]
+        out = []
+        for step in (1, 3, 2):
+            sem = (part, level, step - 1, sems)
+            out.append(
+                go(
+                    copy(
+                        src.at[lax.rem(at[axis] + step, 4)], dst.at[step - 1],
+                        rs_send.at[sem], rs_recv.at[sem], ahead(axis, step),
+                    )
+                )
+            )
+        return out
+
+    def core_sum(part, half, swapped):
+        swapped[part].wait_recv()
+        outer, inner = (2, 4) if part == 2 else (4, 4)
+
+        def add(index, carry):
+            a, b = index // inner, lax.rem(index, inner)
+            total = sbs[part][half, core, a, b].astype(F32) + rbs[part][half, a, b].astype(F32)
+            tot[part][half, a, b] = total.astype(BF16)
+            return carry
+
+        lax.fori_loop(0, outer * inner, add, 0)
+
+    column = []
+    for step in (1, 3, 2):
+        where = moved("y", step)
+        sem = (2, 0, step - 1, 0)
+        c = copy(
+            tot[2].at[where["y"] // 2, lax.rem(where["y"], 2)], ras[2].at[step - 1],
+            rs_send.at[sem], rs_recv.at[sem], device(where, core),
+        )
+        column.append((where["y"] // 2, c))
+
+    def first_sums(half, swapped):
+        out = []
+        core_sum(2, half, swapped)
+        for owner, c in column:
+            pl.when(owner == half)(c.start)
+        for part in range(2):
+            core_sum(part, half, swapped)
+            out.append(scatter(part, 0, tot[part].at[half], ras[part].at[half], half))
+        return out
+
+    def second_sums(part, half, copies):
+        wait_for(copies)
+        mine = at[ORDER[part][2]]
+
+        def add(index, carry):
+            total = tot[part][half, mine, index].astype(F32)
+            for step in range(3):
+                total = total + ras[part][half, step, index].astype(F32)
+            us[part][half, index] = total.astype(BF16)
+            return carry
+
+        lax.fori_loop(0, 4, add, 0)
+        return scatter(part, 1, us[part].at[half], rcs[part].at[half], half)
+
+    def third_sums(part, half, copies):
+        wait_for(copies)
+        total = us[part][half, at[ORDER[part][1]]].astype(F32)
+        for step in range(3):
+            total = total + rcs[part][half, step].astype(F32)
+        vs[part][2 * half : 2 * half + 2] = total.astype(BF16)
+
+    early_swap = swap(EARLY)
+    lax.fori_loop(1, 4, up_layer, 0)
+    early_first = first_sums(EARLY, early_swap)
     up_next.wait_recv()
 
     pick_row = lax.broadcasted_iota(jnp.int32, (288, 128), 0)
@@ -304,107 +413,82 @@
                 if 0 <= depth < 3:
                     first = (sample * 2 + quarter) * 32
                     for tap in range(9):
-                        column = (depth * 9 + tap) * 128
-                        gathered[first : first + 32, column : column + 128] = picked[
-                            tap * 32 : tap * 32 + 32
-                        ]
-    acc = jnp.zeros((128, 256), F32)
+                        columns = slice((depth * 9 + tap) * 128, (depth * 9 + tap) * 128 + 128)
+                        gathered[first : first + 32, columns] = picked[tap * 32 : tap * 32 + 32]
     coarse_t = coarse[...].reshape(128, 256).astype(F32).T.astype(BF16)
     for index in range(9):
-        column = index * 384
-        block = gathered[:, column : column + 384]
-        acc = acc + nt(block, w_up[index])
-        out = nn(coarse_t, block)
+        out = nn(coarse_t, gathered[:, index * 384 : index * 384 + 384])
         for col in range(3):
             start = 2 * FILTER + (index * 3 + col) * 256
             fflat[start : start + 256, :] = out[:, col * 128 : col * 128 + 128]
+    lax.fori_loop(32, 64, pack, 0)
+    late_swap = swap(LATE)
+    for part in range(2):
+        wait_for([core_copy(part, LATE, number, other) for number in range(4)])
+    late_first = first_sums(LATE, late_swap)
+
+    early_second = [second_sums(part, EARLY, early_first[part]) for part in range(2)]
+    lax.fori_loop(32, 64, unpack, 0)
+    taps(w_up, 2 * FILTER, 256)
+    acc = jnp.zeros((128, 256), F32)
+    for index in range(9):
+        acc = acc + nt(gathered[:, index * 384 : index * 384 + 384], w_up[index])
     coarse_grad[...] = acc.astype(BF16)
-
-    def pack(chip, carry):
-        where = place(chip, 0)
-        base = pl.multiple_of(chip * 216, 8)
-        value = fflat[pl.ds(base, 224), :]
-        for which in range(2):
-            for part in range(3):
-                axes = ORDER[part]
-                start = which * ROWS + START[part]
-                rows = value[start : start + HOLD[part]].astype(BF16)
-                sbs[part][which, where[axes[2]], where[axes[1]], where[axes[0]]] = rows
+    for part in range(2):
+        third_sums(part, EARLY, early_second[part])
+
+    for _, c in column:
+        c.wait_recv()
+    mine = (at["y"] // 2, lax.rem(at["y"], 2))
+
+    def add_plane(index, carry):
+        total = tot[2][mine[0], mine[1], index].astype(F32)
+        for step in range(3):
+            total = total + ras[2][step, index].astype(F32)
+        us[2][index] = total.astype(BF16)
         return carry
 
-    lax.fori_loop(0, 64, pack, 0)
-    swaps = [
-        go(copy(sbs[part].at[other], rbs[part], swap_send.at[part], swap_recv.at[part], partner))
-        for part in range(3)
-    ]
-
-    def scatter(part, level, src, dst):
-        axis = ORDER[part][2 - level]
-        out = []
-        for step in (1, 3, 2):
-            sem = (part, level, step - 1)
-            out.append(
-                go(
-                    copy(
-                        src.at[lax.rem(at[axis] + step, 4)], dst.at[step - 1],
-                        rs_send.at[sem], rs_recv.at[sem], ahead(axis, step),
-                    )
-                )
-            )
-        return out
-
-    first = []
-    for part in range(3):
-        swaps[part].wait_recv()
-
-        def add(index, carry, part=part):
-            total = sbs[part][core, index // 4, lax.rem(index, 4)].astype(F32)
-            total = total + rbs[part][index // 4, lax.rem(index, 4)].astype(F32)
-            tot[part][index // 4, lax.rem(index, 4)] = total.astype(BF16)
-            return carry
-
-        lax.fori_loop(0, 16, add, 0)
-        first.append(scatter(part, 0, tot[part], ras[part]))
-    second = []
-    for part in range(3):
-        for c in first[part]:
-            c.wait_recv()
-        mine = at[ORDER[part][2]]
-
-        def add(index, carry, part=part, mine=mine):
-            total = tot[part][mine, index].astype(F32)
-            for step in range(3):
-                total = total + ras[part][step, index].astype(F32)
-            us[part][index] = total.astype(BF16)
-            return carry
-
-        lax.fori_loop(0, 4, add, 0)
-        second.append(scatter(part, 1, us[part], rcs[part]))
-    third = []
-    for part in range(3):
-        for c in second[part]:
-            c.wait_recv()
-        total = us[part][at[ORDER[part][1]]].astype(F32)
-        for step in range(3):
-            total = total + rcs[part][step].astype(F32)
-        vs[part][...] = total.astype(BF16)
-        third.append(scatter(part, 2, vs[part], rds[part]))
-    for part in range(3):
-        for c in third[part]:
-            c.wait_recv()
+    lax.fori_loop(0, 4, add_plane, 0)
+    plane = scatter(2, 1, us[2], rcs[2], 0)
+    late_second = [second_sums(part, LATE, late_first[part]) for part in range(2)]
+    wait_for(plane)
+    total = us[2][at["x"]].astype(F32)
+    for step in range(3):
+        total = total + rcs[2][step].astype(F32)
+    vs[2][...] = total.astype(BF16)
+    last = [None, None, scatter(2, 2, vs[2], rds[2], 0)]
+    for part in range(2):
+        third_sums(part, LATE, late_second[part])
+        last[part] = scatter(part, 2, vs[part], rds[part], 0)
+    for part in (2, 0, 1):
+        wait_for(last[part])
         total = vs[part][at[ORDER[part][0]]].astype(F32)
         for step in range(3):
             total = total + rds[part][step].astype(F32)
         summed[START[part] : START[part] + VALID[part], :] = total[: VALID[part]]
     for c in started:
         c.wait_send()
+    for _, c in column:
+        c.wait_send()
 
 
 def body(coarse_in, pre_up, pre_mid, grad_out, master, moment, second):
     vmem = pl.BlockSpec(memory_space=pltpu.VMEM)
     scratch = []
-    for shape in ((2, 4, 4, 4), (2, 4, 4, 4), (4, 4, 4), (4, 4, 4), (3, 4, 4), (4, 4), (3, 4), (4,), (3,)):
-        scratch += [pltpu.VMEM(shape + (hold, 128), BF16) for hold in HOLD]
+    for shape, column in (
+        ((2, 2, 4, 4, 2), (2, 2, 2, 4, 4)),
+        ((2, 2, 4, 4, 2), (2, 2, 2, 4, 4)),
+        ((2, 4, 4, 2), (2, 2, 4, 4)),
+        ((2, 4, 4, 2), (2, 2, 4, 4)),
+        ((2, 3, 4, 2), (3, 4, 4)),
+        ((2, 4, 2), (4, 4)),
+        ((2, 3, 2), (3, 4)),
+        ((4,), (4,)),
+        ((3,), (3,)),
+    ):
+        for part in range(3):
+            lead = column if part == 2 else shape
+            scratch.append(pltpu.VMEM(lead + (HOLD[part], 128), BF16))
     scratch += [
         pltpu.VMEM((TOTAL, 128), F32),
         pltpu.VMEM((TOTAL + 8, 128), F32),
@@ -420,7 +504,7 @@
         pltpu.VMEM((2, 2, 8, 16, 128), BF16),
         pltpu.VMEM((2, 2, 8, 16, 128), BF16),
     ]
-    for shape in ((3, 3, 3), (3, 7), (3, 3, 3), (3,), (5,)):
+    for shape in ((3, 3, 3, 2), (3, 2, 4), (3, 3, 3, 2), (3, 2), (5,)):
         scratch += [pltpu.SemaphoreType.DMA(shape)] * 2
     coarse_grad, summed = pl.pallas_call(
         kernel,

time: 74.3 us -> 66.4 us (0.89)
  Pallas kernels: 71.3 us -> 63.3 us
    pallas_call x1, Pallas kernels: 71.3 us -> 63.3 us  [body(): pl.pallas_call(kernel, out_shape=(jax.ShapeDtypeStruct((128, 256), BF16),...]
where the time goes in v2:
time: 66.4 us; the launch traced here: 66.2 us
  Pallas kernels  63.3 us (95%)
  other arithmetic  1.53 us (2%)
  between operations  0.7 us (1%)
    pallas_call x1, Pallas kernels, body(): pl.pallas_call(kernel, out_shape=(jax.ShapeDtypeStruct((128, 256), BF16),...  63.3 us
    sub x1, other arithmetic, body(): new_master = master - learn_rate * corrected / scaled  1.53 us

profile of v2, /device:TPU:0, one launch (start us, length us, event | category | flops | bytes accessed | tf_op | source)
XLA Modules:
  0.0 66.2 jit_solution(2901930573773040313)
XLA Ops:
  0.6 0.0 copy-start
  0.6 0.0 copy-start.2
  0.7 0.0 copy-start.3
  0.7 63.3 %shard_map.102 = (bf16[128,256]{1,0:T(8,128)(2,1)}, f32[108,128]{1,0:T(8,128)}) custom-call(f32[108,128]{1,0:T(8,128)} %master.1, bf16[2,4,8,16,128]{4,3,2,1,0:T(8,128)(2,1)} %bitcast.5, bf16[2,4,8,16,128]{4,3,2,1,0:T(8,128)(2,1)} %bitcast.6, bf16[2,4,8,16,128]{4,3,2,1,0:T(8,128)(2,1)} %bitcast.7, bf16[128,256]{1,0:T(8,128)(2,1)} %bitcast.8), custom_call_target="tpu_custom_call" | custom-call | tf_op jit(solution)/shard_map/pallas_call | solution.py:509
  64.0 0.0 copy-done
  64.0 0.0 copy-done.2
  64.0 0.0 copy-done.3
  64.0 0.0 copy-start.1
  64.0 1.5 %divide_subtract_fusion = (f32[108,128]{1,0:T(8,128)}, f32[108,128]{1,0:T(8,128)}, f32[108,128]{1,0:T(8,128)}) fusion(f32[108,128]{1,0:T(8,128)S(1)} %copy-done, f32[108,128]{1,0:T(8,128)} %get-tuple-element.7, f32[108,128]{1,0:T(8,128)S(1)} %copy-done.2, f32[108,128]{1,0:T(8,128)S(1)} %copy-done.3), kind=kLoop, calls=%fused_computation | loop fusion | flops 179712 | bytes 387072 | tf_op jit(solution)/shard_map/sub | solution.py:533
  65.6 0.0 copy-done.1
  65.6 0.6 copy.12
Async XLA Ops:
  0.6 63.4 %copy-start = (f32[108,128]{1,0:T(8,128)S(1)}, f32[108,128]{1,0:T(8,128)}, u32[]{:S(2)}) copy-start(f32[108,128]{1,0:T(8,128)} %master.1) | copy-start | bytes 165892
  0.6 63.4 %copy-start.2 = (f32[108,128]{1,0:T(8,128)S(1)}, f32[108,128]{1,0:T(8,128)}, u32[]{:S(2)}) copy-start(f32[108,128]{1,0:T(8,128)} %param.12) | copy-start | bytes 165892
  0.7 63.4 %copy-start.3 = (f32[108,128]{1,0:T(8,128)S(1)}, f32[108,128]{1,0:T(8,128)}, u32[]{:S(2)}) copy-start(f32[108,128]{1,0:T(8,128)} %param.13) | copy-start | bytes 165892
  64.0 1.5 %copy-start.1 = (bf16[128,256]{1,0:T(8,128)(2,1)S(1)}, bf16[128,256]{1,0:T(8,128)(2,1)}, u32[]{:S(2)}) copy-start(bf16[128,256]{1,0:T(8,128)(2,1)} %get-tuple-element.6) | copy-start | bytes 196612

commit v3 on v2

--- a/solution.py
+++ b/solution.py
@@ -36,13 +36,15 @@
 
 
 def kernel(
+    master_in, grad_out_in, pre_mid_in, pre_up_in, coarse_in,
+    coarse_grad, summed,
     master, grad_out, pre_mid, pre_up, coarse,
-    coarse_grad, summed,
     g0, g1, g2, sb0, sb1, sb2, rb0, rb1, rb2, t0, t1, t2, ra0, ra1, ra2,
     u0, u1, u2, rc0, rc1, rc2, v0, v1, v2, rd0, rd1, rd2,
-    wflat, fflat, w_one, w_two, w_up, x_out, x_mid, act_t, mid_raw, up_raw, gathered, halo_out, halo_mid,
+    wflat, fflat, w_one, w_two, w_up, x_out, x_mid, act_mid, act_up, mid_raw, up_raw, up_before,
+    gathered, lowest, halo_out, halo_mid, halo_up,
     ag_send, ag_recv, core_send, core_recv, rs_send, rs_recv, swap_send, swap_recv,
-    halo_send, halo_recv,
+    halo_send, halo_recv, load_sem, token_sem,
 ):
     gat, sbs, rbs, tot = (g0, g1, g2), (sb0, sb1, sb2), (rb0, rb1, rb2), (t0, t1, t2)
     ras, us, rcs, vs, rds = (
@@ -82,7 +84,7 @@
         )
 
     barrier = pltpu.get_barrier_semaphore()
-    targets = [partner, after, before]
+    targets = [partner]
     targets += [ahead(axis, step) for axis in ("x", "y", "z") for step in (1, 2, 3)]
     for target in targets:
         pl.semaphore_signal(barrier, inc=1, device_id=target, device_id_type=MESH)
@@ -95,6 +97,22 @@
             inner = [where[axes[2]], where[axes[1]], lax.rem(where["y"], 2)]
         return tuple([where["y"] // 2] + lead + inner)
 
+    loads = [
+        pltpu.make_async_copy(src, dst, load_sem.at[number])
+        for number, (src, dst) in enumerate(
+            (
+                (master_in, master),
+                (grad_out_in, grad_out),
+                (pre_mid_in, pre_mid),
+                (pre_up_in, pre_up),
+                (coarse_in, coarse.at[0, :, 0:2]),
+            )
+        )
+    ]
+    for load in loads:
+        load.start()
+
+    loads[0].wait()
     for part in range(3):
         rows = master[START[part] : START[part] + VALID[part], :]
         if HOLD[part] > VALID[part]:
@@ -118,6 +136,9 @@
         if level == 0:
             return gat[part].at[place]
         return gat[part].at[(half,) + place[1 : 5 - level]]
+
+    def back_half(step):
+        return lax.rem(at["y"] + 4 - step, 4) // 2
 
     def gather(part, level, half):
         axis = ORDER[part][level]
@@ -130,6 +151,37 @@
             out.append(copy(dst, dst, ag_send.at[sem], ag_recv.at[sem], partner))
         return out
 
+    tall_half = at["y"] // 2
+    tall = []
+    for step in (1, 3, 2):
+        sem = (2, 2, step - 1, 0)
+        src = piece(2, core, 2, 0, at)
+        dst = piece(2, core, 2, 0, moved("y", 4 - step))
+        tall.append(
+            (
+                step,
+                back_half(step),
+                copy(src, src, ag_send.at[sem], ag_recv.at[sem], ahead("y", step)),
+                copy(dst, dst, ag_send.at[sem], ag_recv.at[sem], partner),
+            )
+        )
+
+    def tall_start(half):
+        for _, _, c, _ in tall:
+            pl.when(tall_half == half)(c.start)
+
+    def tall_forward(half):
+        for step, owner, _, c in tall:
+
+            @pl.when(owner == half)
+            def _():
+                c.wait_recv()
+                core_copy(2, 0, step, core).start()
+
+    def tall_partner(half):
+        for step, owner, _, _ in tall:
+            pl.when(owner == half)(core_copy(2, 0, step, other).wait_recv)
+
     def core_copy(part, half, number, which):
         axis = ORDER[part][2]
         ref = piece(part, which, 2, half, moved(axis, 4 - number))
@@ -141,8 +193,8 @@
             c.wait_recv()
 
     leg = [gather(part, 0, EARLY) for part in range(3)]
-    halo_up = go(copy(grad_out.at[:, 3], halo_out.at[0], halo_send.at[0], halo_recv.at[0], after))
-    halo_down = go(copy(grad_out.at[:, 0], halo_out.at[1], halo_send.at[1], halo_recv.at[1], before))
+    for step in (1, 3, 2):
+        pl.semaphore_signal(token_sem.at[0], inc=1, device_id=ahead("z", step), device_id_type=MESH)
 
     row = lax.broadcasted_iota(jnp.int32, (128, 128), 0)
     lane = lax.broadcasted_iota(jnp.int32, (128, 128), 1)
@@ -160,18 +212,27 @@
         )
         ext[sample, layer, 1:9] = wide.reshape(8, 16, 384)
 
-    def transposed_act(pre):
+    def turn(act_t, first, value):
+        turned = jnp.maximum(value, 0.0).T
+        columns = slice(first * 128, first * 128 + 128)
+        low = jnp.where(lane < 16, 0.0, pltpu.roll(turned, 16, 1))
+        high = jnp.where(lane >= 112, 0.0, pltpu.roll(turned, 112, 1))
+        act_t[0:128, columns] = low.astype(BF16)
+        act_t[128:256, columns] = turned.astype(BF16)
+        act_t[256:384, columns] = high.astype(BF16)
+
+    def transposed_act(act_t, pre, depth, first):
         for sample in range(2):
             for layer in range(4):
-                value = jnp.maximum(pre[sample, layer].reshape(128, 128).astype(F32), 0.0)
-                turned = value.T
-                first = sample * 4 + layer
-                columns = slice(first * 128, first * 128 + 128)
-                low = jnp.where(lane < 16, 0.0, pltpu.roll(turned, 16, 1))
-                high = jnp.where(lane >= 112, 0.0, pltpu.roll(turned, 112, 1))
-                act_t[0:128, columns] = low.astype(BF16)
-                act_t[128:256, columns] = turned.astype(BF16)
-                act_t[256:384, columns] = high.astype(BF16)
+                value = pre[sample, layer].reshape(128, 128).astype(F32)
+                turn(act_t, sample * depth + first + layer, value)
+
+    def transposed_edges(act_t, halo):
+        for sample in range(2):
+            low = halo[0, sample].reshape(128, 128).astype(F32)
+            turn(act_t, sample * 6, jnp.where(slab > 0, low, 0.0))
+            high = halo[1, sample].reshape(128, 128).astype(F32)
+            turn(act_t, sample * 6 + 5, jnp.where(slab < 31, high, 0.0))
 
     def own_layers(index, carry):
         sample, layer = index // 4, lax.rem(index, 4)
@@ -185,9 +246,18 @@
             high = halo[1, sample].reshape(128, 128).astype(F32)
             widen(ext, sample, 5, jnp.where(slab < 31, high, 0.0))
 
-    def filter_grad(ext, first, depth):
+    def grad_by_cotangent(ext, act_t, first, depth):
         right = ext[:, 2 - depth : 6 - depth, 1:9].reshape(1024, 384)
-        out = nn(act_t[...], right)
+        store_grad(first, depth, nn(act_t[...], right))
+
+    def grad_by_act(ext, act_t, first, depth):
+        out = jnp.zeros((384, 384), F32)
+        for sample in range(2):
+            start = (sample * 6 + depth) * 128
+            out = out + nn(act_t[:, start : start + 512], ext[sample, 1:5, 1:9].reshape(512, 384))
+        store_grad(first, depth, out)
+
+    def store_grad(first, depth, out):
         for height in range(3):
             for col in range(3):
                 start = first + ((depth * 3 + height) * 3 + col) * 128
@@ -237,23 +307,53 @@
                 sbs[part][block(sbs[part], part, [which], where)] = rows
         return carry
 
-    transposed_act(pre_mid)
+    def pack_late(chip, carry):
+        where = place(chip)
+        base = pl.multiple_of(chip * 216, 8)
+        value = fflat[pl.ds(base, 224), :]
+        value = jnp.where(core == 0, value[0:112], value[ROWS : ROWS + 112])
+        for part in range(3):
+            rows = value[START[part] : START[part] + HOLD[part]].astype(BF16)
+            tot[part][block(tot[part], part, [], where)] = rows
+        return carry
+
+    for load in loads[1:]:
+        load.wait()
+    transposed_act(act_mid, pre_mid, 4, 0)
     for part in range(3):
         wait_for(leg[part])
     leg = [gather(part, 1, EARLY) for part in range(3)]
-    later_leg = [gather(part, 1, LATE) for part in range(2)]
+    pl.semaphore_wait(token_sem.at[0], 3)
+    pl.semaphore_signal(token_sem.at[1], inc=1, device_id=ahead("y", 2), device_id_type=MESH)
     lax.fori_loop(0, 8, own_layers, 0)
-    filter_grad(x_out, FILTER, 1)
+    grad_by_cotangent(x_out, act_mid, FILTER, 1)
+    pl.semaphore_wait(token_sem.at[1], 1)
+    halos = []
+    for number, (src, dst, target) in enumerate(
+        (
+            (grad_out.at[:, 3], halo_out.at[0], after),
+            (grad_out.at[:, 0], halo_out.at[1], before),
+            (pre_up.at[:, 3], halo_up.at[0], after),
+            (pre_up.at[:, 0], halo_up.at[1], before),
+            (coarse.at[0, :, 0], coarse.at[0, :, 2], before),
+        )
+    ):
+        sem = 3 + number
+        halos.append(go(copy(src, dst, halo_send.at[sem], halo_recv.at[sem], target)))
     third = []
-    for part in range(3):
+    for part in (2, 0, 1):
         wait_for(leg[part])
-        third.append(gather(part, 2, EARLY))
+        if part == 2:
+            tall_start(EARLY)
+        else:
+            third.append(gather(part, 2, EARLY))
         go(core_copy(part, EARLY, 0, core))
-    halo_up.wait_recv()
-    halo_down.wait_recv()
+    leg = [gather(part, 1, LATE) for part in range(2)]
+    transposed_act(act_up, pre_up, 6, 1)
+    wait_for(halos[0:2])
     edges(x_out, halo_out)
-    filter_grad(x_out, FILTER, 0)
-    filter_grad(x_out, FILTER, 2)
+    grad_by_cotangent(x_out, act_mid, FILTER, 0)
+    grad_by_cotangent(x_out, act_mid, FILTER, 2)
     lax.fori_loop(16, 32, pack, 0)
 
     def forward(part, half, copies):
@@ -261,56 +361,19 @@
             c.wait_recv()
             go(core_copy(part, half, step, core))
 
-    for part in range(3):
+    tall_forward(EARLY)
+    for part in range(2):
         forward(part, EARLY, third[part])
-    late_third = []
+    third = []
     for part in range(2):
-        wait_for(later_leg[part])
-        late_third.append(gather(part, 2, LATE))
+        wait_for(leg[part])
+        third.append(gather(part, 2, LATE))
         go(core_copy(part, LATE, 0, core))
-    for part in range(3):
+    tall_start(LATE)
+    core_copy(2, EARLY, 0, other).wait_recv()
+    tall_partner(EARLY)
+    for part in range(2):
         wait_for([core_copy(part, EARLY, number, other) for number in range(4)])
-
-    lax.fori_loop(16, 32, unpack, 0)
-    taps(w_two, FILTER, 128)
-
-    def mid_layer(index, carry):
-        layer = lax.rem(index + 3, 4)
-        value = back_conv(x_out, w_two, layer)
-        keep = pre_mid[:, layer].reshape(256, 128).astype(F32) > 0.0
-        value = jnp.where(keep, value, 0.0).astype(BF16)
-        mid_raw[:, layer] = value.reshape(2, 8, 16, 128)
-        for sample in range(2):
-            widen(x_mid, sample, layer + 1, value[sample * 128 : sample * 128 + 128].astype(F32))
-        return carry
-
-    lax.fori_loop(0, 2, mid_layer, 0)
-    mid_up = go(copy(mid_raw.at[:, 3], halo_mid.at[0], halo_send.at[2], halo_recv.at[2], after))
-    mid_down = go(copy(mid_raw.at[:, 0], halo_mid.at[1], halo_send.at[3], halo_recv.at[3], before))
-    lax.fori_loop(2, 4, mid_layer, 0)
-    lax.fori_loop(0, 16, unpack, 0)
-    taps(w_one, 0, 128)
-    transposed_act(pre_up)
-    filter_grad(x_mid, 0, 1)
-    for part in range(2):
-        forward(part, LATE, late_third[part])
-    mid_up.wait_recv()
-    mid_down.wait_recv()
-    edges(x_mid, halo_mid)
-
-    def up_layer(index, carry):
-        layer = lax.rem(index + 3, 4)
-        value = back_conv(x_mid, w_one, layer)
-        keep = pre_up[:, layer].reshape(256, 128).astype(F32) > 0.0
-        value = jnp.where(keep, value, 0.0).astype(BF16)
-        up_raw[:, layer + 1] = value.reshape(2, 128, 128)
-        return carry
-
-    lax.fori_loop(0, 1, up_layer, 0)
-    up_next = go(copy(up_raw.at[:, 4], up_raw.at[:, 0], halo_send.at[4], halo_recv.at[4], after))
-    filter_grad(x_mid, 0, 0)
-    filter_grad(x_mid, 0, 2)
-    lax.fori_loop(0, 16, pack, 0)
 
     def swap(half):
         return [
@@ -322,6 +385,51 @@
             )
             for part in range(3)
         ]
+
+    lax.fori_loop(16, 32, unpack, 0)
+    taps(w_two, FILTER, 128)
+
+    def mid_layer(index, carry):
+        layer = lax.rem(index + 3, 4)
+        value = back_conv(x_out, w_two, layer)
+        keep = pre_mid[:, layer].reshape(256, 128).astype(F32) > 0.0
+        value = jnp.where(keep, value, 0.0).astype(BF16)
+        mid_raw[:, layer] = value.reshape(2, 8, 16, 128)
+        for sample in range(2):
+            widen(x_mid, sample, layer + 1, value[sample * 128 : sample * 128 + 128].astype(F32))
+        return carry
+
+    lax.fori_loop(0, 2, mid_layer, 0)
+    mid_up = go(copy(mid_raw.at[:, 3], halo_mid.at[0], halo_send.at[0], halo_recv.at[0], after))
+    mid_down = go(copy(mid_raw.at[:, 0], halo_mid.at[1], halo_send.at[1], halo_recv.at[1], before))
+    lax.fori_loop(2, 4, mid_layer, 0)
+    lax.fori_loop(0, 16, unpack, 0)
+    taps(w_one, 0, 128)
+    wait_for(halos[2:])
+    pair = go(copy(coarse.at[0], coarse.at[1], halo_send.at[8], halo_recv.at[8], partner))
+    transposed_edges(act_up, halo_up)
+    for depth in range(3):
+        grad_by_act(x_mid, act_up, 0, depth)
+    lax.fori_loop(0, 16, pack, 0)
+    early_swap = swap(EARLY)
+    tall_forward(LATE)
+    for part in range(2):
+        forward(part, LATE, third[part])
+    mid_up.wait_recv()
+    mid_down.wait_recv()
+    edges(x_mid, halo_mid)
+
+    def up_layer(index, carry):
+        layer = lax.rem(index + 3, 4)
+        value = back_conv(x_mid, w_one, layer)
+        keep = pre_up[:, layer].reshape(256, 128).astype(F32) > 0.0
+        value = jnp.where(keep, value, 0.0).astype(BF16)
+        up_raw[0, :, layer] = value.reshape(2, 128, 128)
+        return carry
+
+    lax.fori_loop(0, 4, up_layer, 0)
+    up_pair = go(copy(up_raw.at[0], up_raw.at[1], halo_send.at[2], halo_recv.at[2], partner))
+    up_next = go(copy(up_raw.at[0, :, 3], up_before, halo_send.at[9], halo_recv.at[9], after))
 
     def scatter(part, level, src, dst, sems):
         axis = ORDER[part][2 - level]
@@ -360,15 +468,10 @@
         )
         column.append((where["y"] // 2, c))
 
-    def first_sums(half, swapped):
-        out = []
-        core_sum(2, half, swapped)
+    def first_sends(half):
         for owner, c in column:
             pl.when(owner == half)(c.start)
-        for part in range(2):
-            core_sum(part, half, swapped)
-            out.append(scatter(part, 0, tot[part].at[half], ras[part].at[half], half))
-        return out
+        return [scatter(part, 0, tot[part].at[half], ras[part].at[half], half) for part in range(2)]
 
     def second_sums(part, half, copies):
         wait_for(copies)
@@ -391,10 +494,9 @@
             total = total + rcs[part][half, step].astype(F32)
         vs[part][2 * half : 2 * half + 2] = total.astype(BF16)
 
-    early_swap = swap(EARLY)
-    lax.fori_loop(1, 4, up_layer, 0)
-    early_first = first_sums(EARLY, early_swap)
-    up_next.wait_recv()
+    for part in (2, 0, 1):
+        core_sum(part, EARLY, early_swap)
+    early_first = first_sends(EARLY)
 
     pick_row = lax.broadcasted_iota(jnp.int32, (288, 128), 0)
     pick_lane = lax.broadcasted_iota(jnp.int32, (288, 128), 1)
@@ -403,36 +505,67 @@
     fine_col = 2 * coarse_col + lax.rem(tap, 3) - 1
     chosen = (fine_row >= 0) & (fine_col >= 0) & (pick_lane == fine_row * 16 + fine_col)
     pick = jnp.where(chosen, 1.0, 0.0).astype(BF16)
+
+    def spread(slot, sample, layer):
+        picked = nn(pick, up_raw[slot, sample, layer]).astype(BF16)
+        first = ((slot * 2 + sample) * 2 + layer // 2) * 32
+        for depth in (1,) if layer % 2 == 0 else (0, 2):
+            for tap in range(9):
+                columns = slice((depth * 9 + tap) * 128, (depth * 9 + tap) * 128 + 128)
+                gathered[first : first + 32, columns] = picked[tap * 32 : tap * 32 + 32]
+        return picked
+
+    def lower(sample, quarter, picked):
+        first = (sample * 2 + quarter) * 32
+        for tap in range(9):
+            lowest[first : first + 32, tap * 128 : tap * 128 + 128] = picked[tap * 32 : tap * 32 + 32]
+
     for sample in range(2):
-        for layer in range(5):
-            value = up_raw[sample, layer]
-            if layer == 0:
-                value = jnp.where(slab > 0, value.astype(F32), 0.0).astype(BF16)
-            picked = nn(pick, value).astype(BF16)
-            for depth, quarter in ((layer, 0), (layer - 2, 1)):
-                if 0 <= depth < 3:
-                    first = (sample * 2 + quarter) * 32
-                    for tap in range(9):
-                        columns = slice((depth * 9 + tap) * 128, (depth * 9 + tap) * 128 + 128)
-                        gathered[first : first + 32, columns] = picked[tap * 32 : tap * 32 + 32]
-    coarse_t = coarse[...].reshape(128, 256).astype(F32).T.astype(BF16)
+        for layer in range(4):
+            picked = spread(0, sample, layer)
+            if layer == 1:
+                lower(sample, 1, picked)
+    pair.wait_recv()
+    turned = []
+    for first in (1, 0):
+        rows = []
+        for slot in range(2):
+            for sample in range(2):
+                for quarter in (first, first + 1):
+                    value = coarse[slot, sample, quarter].astype(F32)
+                    if quarter == 2:
+                        value = jnp.where(slab < 31, value, 0.0)
+                    rows.append(value)
+        turned.append(jnp.concatenate(rows, axis=0).T.astype(BF16))
+    up_pair.wait_recv()
+    for sample in range(2):
+        for layer in range(4):
+            spread(1, sample, layer)
     for index in range(9):
-        out = nn(coarse_t, gathered[:, index * 384 : index * 384 + 384])
+        out = nn(turned[min(index // 3, 1)], gathered[:, index * 384 : index * 384 + 384])
         for col in range(3):
             start = 2 * FILTER + (index * 3 + col) * 256
             fflat[start : start + 256, :] = out[:, col * 128 : col * 128 + 128]
-    lax.fori_loop(32, 64, pack, 0)
-    late_swap = swap(LATE)
+    lax.fori_loop(32, 64, pack_late, 0)
+    late_first = first_sends(LATE)
+
+    tall_partner(LATE)
     for part in range(2):
         wait_for([core_copy(part, LATE, number, other) for number in range(4)])
-    late_first = first_sums(LATE, late_swap)
-
     early_second = [second_sums(part, EARLY, early_first[part]) for part in range(2)]
     lax.fori_loop(32, 64, unpack, 0)
     taps(w_up, 2 * FILTER, 256)
+    up_next.wait_recv()
+    for sample in range(2):
+        value = jnp.where(slab > 0, up_before[sample].astype(F32), 0.0).astype(BF16)
+        lower(sample, 0, nn(pick, value).astype(BF16))
     acc = jnp.zeros((128, 256), F32)
     for index in range(9):
-        acc = acc + nt(gathered[:, index * 384 : index * 384 + 384], w_up[index])
+        if index < 3:
+            left = lowest[:, index * 384 : index * 384 + 384]
+        else:
+            left = gathered[0:128, index * 384 : index * 384 + 384]
+        acc = acc + nt(left, w_up[index])
     coarse_grad[...] = acc.astype(BF16)
     for part in range(2):
         third_sums(part, EARLY, early_second[part])
@@ -470,11 +603,21 @@
         c.wait_send()
     for _, c in column:
         c.wait_send()
+    for step, _, c, _ in tall:
+        c.wait_send()
+        core_copy(2, 0, step, core).wait_send()
 
 
 def body(coarse_in, pre_up, pre_mid, grad_out, master, moment, second):
     vmem = pl.BlockSpec(memory_space=pltpu.VMEM)
-    scratch = []
+    held = pl.BlockSpec(memory_space=pl.ANY)
+    scratch = [
+        pltpu.VMEM((ROWS, 128), F32),
+        pltpu.VMEM((2, 4, 8, 16, 128), BF16),
+        pltpu.VMEM((2, 4, 8, 16, 128), BF16),
+        pltpu.VMEM((2, 4, 8, 16, 128), BF16),
+        pltpu.VMEM((2, 2, 3, 32, 256), BF16),
+    ]
     for shape, column in (
         ((2, 2, 4, 4, 2), (2, 2, 2, 4, 4)),
         ((2, 2, 4, 4, 2), (2, 2, 2, 4, 4)),
@@ -498,21 +641,26 @@
         pltpu.VMEM((2, 6, 10, 16, 384), BF16),
         pltpu.VMEM((2, 6, 10, 16, 384), BF16),
         pltpu.VMEM((384, 1024), BF16),
+        pltpu.VMEM((384, 1536), BF16),
         pltpu.VMEM((2, 4, 8, 16, 128), BF16),
-        pltpu.VMEM((2, 5, 128, 128), BF16),
-        pltpu.VMEM((128, FILTER), BF16),
+        pltpu.VMEM((2, 2, 4, 128, 128), BF16),
+        pltpu.VMEM((2, 128, 128), BF16),
+        pltpu.VMEM((256, FILTER), BF16),
+        pltpu.VMEM((128, 9 * 128), BF16),
+        pltpu.VMEM((2, 2, 8, 16, 128), BF16),
         pltpu.VMEM((2, 2, 8, 16, 128), BF16),
         pltpu.VMEM((2, 2, 8, 16, 128), BF16),
     ]
-    for shape in ((3, 3, 3, 2), (3, 2, 4), (3, 3, 3, 2), (3, 2), (5,)):
+    for shape in ((3, 3, 3, 2), (3, 2, 4), (3, 3, 3, 2), (3, 2), (10,)):
         scratch += [pltpu.SemaphoreType.DMA(shape)] * 2
+    scratch += [pltpu.SemaphoreType.DMA((5,)), pltpu.SemaphoreType.REGULAR((2,))]
     coarse_grad, summed = pl.pallas_call(
         kernel,
         out_shape=(
             jax.ShapeDtypeStruct((128, 256), BF16),
             jax.ShapeDtypeStruct((ROWS, 128), F32),
         ),
-        in_specs=[vmem] * 5,
+        in_specs=[held] * 5,
         out_specs=(vmem, vmem),
         scratch_shapes=scratch,
         compiler_params=pltpu.CompilerParams(
@@ -523,7 +671,7 @@
         grad_out.reshape(grad_out.shape[1:]),
         pre_mid.reshape(pre_mid.shape[1:]),
         pre_up.reshape(pre_up.shape[1:]),
-        coarse_in.reshape(128, 256),
+        coarse_in.reshape(2, 2, 32, 256),
     )
     mean_grad = summed / 8.0
     new_moment = beta_one * moment + (1.0 - beta_one) * mean_grad

time: 66.4 us -> 63.9 us (0.962)
  Pallas kernels: 63.3 us -> 60.8 us
    pallas_call x1, Pallas kernels: 63.3 us -> 60.8 us  [body(): pl.pallas_call(kernel, out_shape=(jax.ShapeDtypeStruct((128, 256), BF16),...]
where the time goes in v3:
time: 63.9 us; the launch traced here: 63.7 us
  Pallas kernels  60.8 us (95%)
  other arithmetic  1.53 us (2%)
  between operations  0.7 us (1%)
  local copies, waits for them, and re-layouts  0.65 us (1%)
    pallas_call x1, Pallas kernels, body(): pl.pallas_call(kernel, out_shape=(jax.ShapeDtypeStruct((128, 256), BF16),...  60.8 us
    sub x1, other arithmetic, body(): new_master = master - learn_rate * corrected / scaled  1.53 us

profile of v3, /device:TPU:0, one launch (start us, length us, event | category | flops | bytes accessed | tf_op | source)
XLA Modules:
  0.0 63.7 jit_solution(12203326924517536760)
XLA Ops:
  0.6 0.0 copy-start
  0.6 0.0 copy-start.2
  0.7 0.0 copy-start.3
  0.7 60.8 %shard_map.102 = (bf16[128,256]{1,0:T(8,128)(2,1)}, f32[108,128]{1,0:T(8,128)}) custom-call(f32[108,128]{1,0:T(8,128)} %master_in.1, bf16[2,4,8,16,128]{4,3,2,1,0:T(8,128)(2,1)} %bitcast.5, bf16[2,4,8,16,128]{4,3,2,1,0:T(8,128)(2,1)} %bitcast.6, bf16[2,4,8,16,128]{4,3,2,1,0:T(8,128)(2,1)} %bitcast.7, bf16[2,2,32,256]{3,2,1,0:T(8,128)(2,1)} %bitcast.8), custom_call_target="tpu_custom_call" | custom-call | tf_op jit(solution)/shard_map/pallas_call | solution.py:657
  61.5 0.0 copy-done
  61.5 0.0 copy-done.2
  61.5 0.0 copy-done.3
  61.5 0.0 copy-start.1
  61.5 1.5 %divide_subtract_fusion = (f32[108,128]{1,0:T(8,128)}, f32[108,128]{1,0:T(8,128)}, f32[108,128]{1,0:T(8,128)}) fusion(f32[108,128]{1,0:T(8,128)S(1)} %copy-done, f32[108,128]{1,0:T(8,128)} %get-tuple-element.7, f32[108,128]{1,0:T(8,128)S(1)} %copy-done.2, f32[108,128]{1,0:T(8,128)S(1)} %copy-done.3), kind=kLoop, calls=%fused_computation | loop fusion | flops 179712 | bytes 387072 | tf_op jit(solution)/shard_map/sub | solution.py:681
  63.1 0.0 copy-done.1
  63.1 0.6 copy.12
Async XLA Ops:
  0.6 60.9 %copy-start = (f32[108,128]{1,0:T(8,128)S(1)}, f32[108,128]{1,0:T(8,128)}, u32[]{:S(2)}) copy-start(f32[108,128]{1,0:T(8,128)} %master_in.1) | copy-start | bytes 165892
  0.6 60.9 %copy-start.2 = (f32[108,128]{1,0:T(8,128)S(1)}, f32[108,128]{1,0:T(8,128)}, u32[]{:S(2)}) copy-start(f32[108,128]{1,0:T(8,128)} %param.12) | copy-start | bytes 165892
  0.7 60.9 %copy-start.3 = (f32[108,128]{1,0:T(8,128)S(1)}, f32[108,128]{1,0:T(8,128)}, u32[]{:S(2)}) copy-start(f32[108,128]{1,0:T(8,128)} %param.13) | copy-start | bytes 165892
  61.5 1.5 %copy-start.1 = (bf16[128,256]{1,0:T(8,128)(2,1)S(1)}, bf16[128,256]{1,0:T(8,128)(2,1)}, u32[]{:S(2)}) copy-start(bf16[128,256]{1,0:T(8,128)(2,1)} %get-tuple-element.6) | copy-start | bytes 196612

commit v4 on v3

--- a/solution.py
+++ b/solution.py
@@ -265,11 +265,14 @@
                     height * 128 : height * 128 + 128, col * 128 : col * 128 + 128
                 ]
 
-    def back_conv(ext, weight, layer):
-        acc = jnp.zeros((256, 128), F32)
+    def back_conv(ext, weight, layers):
+        acc = jnp.zeros((512, 128), F32)
         for depth in range(3):
             for height in range(3):
-                left = ext[:, layer + 2 - depth, 2 - height : 10 - height].reshape(256, 384)
+                rows = slice(2 - height, 10 - height)
+                left = jnp.concatenate(
+                    [ext[:, layer + 2 - depth, rows].reshape(256, 384) for layer in layers], axis=0
+                )
                 acc = acc + nt(left, weight[depth * 3 + height])
         return acc
 
@@ -304,7 +307,7 @@
             for part in range(3):
                 start = which * ROWS + START[part]
                 rows = value[start : start + HOLD[part]].astype(BF16)
-                sbs[part][block(sbs[part], part, [which], where)] = rows
+                sbs[part][block(sbs[part], part, [which], where)[1:]] = rows
         return carry
 
     def pack_late(chip, carry):
@@ -316,6 +319,95 @@
             rows = value[START[part] : START[part] + HOLD[part]].astype(BF16)
             tot[part][block(tot[part], part, [], where)] = rows
         return carry
+
+    def swap(first):
+        out = []
+        for part in range(3):
+            group = pl.ds(first, 2)
+            if part == 0:
+                src, dst = sbs[0].at[other, group], rbs[0].at[group]
+            else:
+                src, dst = sbs[part].at[other, :, group], rbs[part].at[:, group]
+            sem = (part, first // 2)
+            out.append(go(copy(src, dst, swap_send.at[sem], swap_recv.at[sem], partner)))
+        return out
+
+    def core_sums(first, swapped):
+        for part in range(3):
+            swapped[part].wait_recv()
+
+            def add(index, carry, part=part):
+                if part == 0:
+                    a, b = first + index // 4, lax.rem(index, 4)
+                else:
+                    a, b = index // 2, first + lax.rem(index, 2)
+                total = sbs[part][core, a, b].astype(F32) + rbs[part][a, b].astype(F32)
+                tot[part][EARLY, a, b] = total.astype(BF16)
+                return carry
+
+            lax.fori_loop(0, (8, 8, 4)[part], add, 0)
+
+    def scatter(part, level, src, dst, sems):
+        axis = ORDER[part][2 - level]
+        out = []
+        for step in (1, 3, 2):
+            sem = (part, level, step - 1, sems)
+            out.append(
+                go(
+                    copy(
+                        src.at[lax.rem(at[axis] + step, 4)], dst.at[step - 1],
+                        rs_send.at[sem], rs_recv.at[sem], ahead(axis, step),
+                    )
+                )
+            )
+        return out
+
+    early_x, early_z, column = [], [], []
+    for step in (1, 3, 2):
+        where = moved("x", step)
+        sem = (0, 0, step - 1, 0)
+        c = copy(
+            tot[0].at[EARLY, where["x"]], ras[0].at[EARLY, step - 1],
+            rs_send.at[sem], rs_recv.at[sem], device(where, core),
+        )
+        early_x.append((where["x"] // 2 * 2, c))
+        where = moved("y", step)
+        owner = where["y"] // 2
+        for number, group in enumerate((pl.ds(2, 2), pl.ds(0, 2), pl.ds(0, 4))):
+            sem = (2, 0, step - 1, number)
+            c = copy(
+                tot[2].at[where["y"] // 2, lax.rem(where["y"], 2), group],
+                ras[2].at[step - 1, group],
+                rs_send.at[sem], rs_recv.at[sem], device(where, core),
+            )
+            column.append((number, owner, c))
+
+    def early_sends(first):
+        number = 1 - first // 2
+        for owner, c in early_x:
+            pl.when(owner == first)(c.start)
+        group = pl.ds(first, 2)
+        for step in (1, 3, 2):
+            where = moved("z", step)
+            sem = (1, 0, step - 1, number)
+            early_z.append(
+                go(
+                    copy(
+                        tot[1].at[EARLY, where["z"], group], ras[1].at[EARLY, step - 1, group],
+                        rs_send.at[sem], rs_recv.at[sem], device(where, core),
+                    )
+                )
+            )
+        for which, owner, c in column:
+            if which == number:
+                pl.when(owner == EARLY)(c.start)
+
+    def late_sends():
+        out = [scatter(part, 0, tot[part].at[LATE], ras[part].at[LATE], 2) for part in range(2)]
+        for which, owner, c in column:
+            if which == 2:
+                pl.when(owner == LATE)(c.start)
+        return out
 
     for load in loads[1:]:
         load.wait()
@@ -355,6 +447,7 @@
     grad_by_cotangent(x_out, act_mid, FILTER, 0)
     grad_by_cotangent(x_out, act_mid, FILTER, 2)
     lax.fori_loop(16, 32, pack, 0)
+    two_swap = swap(2)
 
     def forward(part, half, copies):
         for step, c in zip((1, 3, 2), copies):
@@ -375,34 +468,25 @@
     for part in range(2):
         wait_for([core_copy(part, EARLY, number, other) for number in range(4)])
 
-    def swap(half):
-        return [
-            go(
-                copy(
-                    sbs[part].at[half, other], rbs[part].at[half],
-                    swap_send.at[part, half], swap_recv.at[part, half], partner,
-                )
-            )
-            for part in range(3)
-        ]
-
     lax.fori_loop(16, 32, unpack, 0)
     taps(w_two, FILTER, 128)
 
-    def mid_layer(index, carry):
-        layer = lax.rem(index + 3, 4)
-        value = back_conv(x_out, w_two, layer)
-        keep = pre_mid[:, layer].reshape(256, 128).astype(F32) > 0.0
-        value = jnp.where(keep, value, 0.0).astype(BF16)
-        mid_raw[:, layer] = value.reshape(2, 8, 16, 128)
-        for sample in range(2):
-            widen(x_mid, sample, layer + 1, value[sample * 128 : sample * 128 + 128].astype(F32))
-        return carry
-
-    lax.fori_loop(0, 2, mid_layer, 0)
+    def mid_layers(layers):
+        both = back_conv(x_out, w_two, layers)
+        for number, layer in enumerate(layers):
+            value = both[number * 256 : number * 256 + 256]
+            keep = pre_mid[:, layer].reshape(256, 128).astype(F32) > 0.0
+            value = jnp.where(keep, value, 0.0).astype(BF16)
+            mid_raw[:, layer] = value.reshape(2, 8, 16, 128)
+            for sample in range(2):
+                widen(x_mid, sample, layer + 1, value[sample * 128 : sample * 128 + 128].astype(F32))
+
+    mid_layers((3, 0))
     mid_up = go(copy(mid_raw.at[:, 3], halo_mid.at[0], halo_send.at[0], halo_recv.at[0], after))
     mid_down = go(copy(mid_raw.at[:, 0], halo_mid.at[1], halo_send.at[1], halo_recv.at[1], before))
-    lax.fori_loop(2, 4, mid_layer, 0)
+    core_sums(2, two_swap)
+    early_sends(2)
+    mid_layers((1, 2))
     lax.fori_loop(0, 16, unpack, 0)
     taps(w_one, 0, 128)
     wait_for(halos[2:])
@@ -411,67 +495,25 @@
     for depth in range(3):
         grad_by_act(x_mid, act_up, 0, depth)
     lax.fori_loop(0, 16, pack, 0)
-    early_swap = swap(EARLY)
+    one_swap = swap(0)
     tall_forward(LATE)
     for part in range(2):
         forward(part, LATE, third[part])
     mid_up.wait_recv()
     mid_down.wait_recv()
+    core_sums(0, one_swap)
+    early_sends(0)
     edges(x_mid, halo_mid)
 
-    def up_layer(index, carry):
-        layer = lax.rem(index + 3, 4)
-        value = back_conv(x_mid, w_one, layer)
-        keep = pre_up[:, layer].reshape(256, 128).astype(F32) > 0.0
-        value = jnp.where(keep, value, 0.0).astype(BF16)
-        up_raw[0, :, layer] = value.reshape(2, 128, 128)
-        return carry
-
-    lax.fori_loop(0, 4, up_layer, 0)
+    for layers in ((3, 0), (1, 2)):
+        both = back_conv(x_mid, w_one, layers)
+        for number, layer in enumerate(layers):
+            value = both[number * 256 : number * 256 + 256]
+            keep = pre_up[:, layer].reshape(256, 128).astype(F32) > 0.0
+            value = jnp.where(keep, value, 0.0).astype(BF16)
+            up_raw[0, :, layer] = value.reshape(2, 128, 128)
     up_pair = go(copy(up_raw.at[0], up_raw.at[1], halo_send.at[2], halo_recv.at[2], partner))
     up_next = go(copy(up_raw.at[0, :, 3], up_before, halo_send.at[9], halo_recv.at[9], after))
-
-    def scatter(part, level, src, dst, sems):
-        axis = ORDER[part][2 - level]
-        out = []
-        for step in (1, 3, 2):
-            sem = (part, level, step - 1, sems)
-            out.append(
-                go(
-                    copy(
-                        src.at[lax.rem(at[axis] + step, 4)], dst.at[step - 1],
-                        rs_send.at[sem], rs_recv.at[sem], ahead(axis, step),
-                    )
-                )
-            )
-        return out
-
-    def core_sum(part, half, swapped):
-        swapped[part].wait_recv()
-        outer, inner = (2, 4) if part == 2 else (4, 4)
-
-        def add(index, carry):
-            a, b = index // inner, lax.rem(index, inner)
-            total = sbs[part][half, core, a, b].astype(F32) + rbs[part][half, a, b].astype(F32)
-            tot[part][half, a, b] = total.astype(BF16)
-            return carry
-
-        lax.fori_loop(0, outer * inner, add, 0)
-
-    column = []
-    for step in (1, 3, 2):
-        where = moved("y", step)
-        sem = (2, 0, step - 1, 0)
-        c = copy(
-            tot[2].at[where["y"] // 2, lax.rem(where["y"], 2)], ras[2].at[step - 1],
-            rs_send.at[sem], rs_recv.at[sem], device(where, core),
-        )
-        column.append((where["y"] // 2, c))
-
-    def first_sends(half):
-        for owner, c in column:
-            pl.when(owner == half)(c.start)
-        return [scatter(part, 0, tot[part].at[half], ras[part].at[half], half) for part in range(2)]
 
     def second_sums(part, half, copies):
         wait_for(copies)
@@ -493,10 +535,6 @@
         for step in range(3):
             total = total + rcs[part][half, step].astype(F32)
         vs[part][2 * half : 2 * half + 2] = total.astype(BF16)
-
-    for part in (2, 0, 1):
-        core_sum(part, EARLY, early_swap)
-    early_first = first_sends(EARLY)
 
     pick_row = lax.broadcasted_iota(jnp.int32, (288, 128), 0)
     pick_lane = lax.broadcasted_iota(jnp.int32, (288, 128), 1)
@@ -547,7 +585,8 @@
             start = 2 * FILTER + (index * 3 + col) * 256
             fflat[start : start + 256, :] = out[:, col * 128 : col * 128 + 128]
     lax.fori_loop(32, 64, pack_late, 0)
-    late_first = first_sends(LATE)
+    late_first = late_sends()
+    early_first = ([c for _, c in early_x], early_z)
 
     tall_partner(LATE)
     for part in range(2):
@@ -570,8 +609,8 @@
     for part in range(2):
         third_sums(part, EARLY, early_second[part])
 
-    for _, c in column:
-        c.wait_recv()
+    for which, _, c in column:
+        pl.when(tall_half == (LATE if which == 2 else EARLY))(c.wait_recv)
     mine = (at["y"] // 2, lax.rem(at["y"], 2))
 
     def add_plane(index, carry):
@@ -601,8 +640,10 @@
         summed[START[part] : START[part] + VALID[part], :] = total[: VALID[part]]
     for c in started:
         c.wait_send()
-    for _, c in column:
+    for _, c in early_x:
         c.wait_send()
+    for which, owner, c in column:
+        pl.when(owner == (LATE if which == 2 else EARLY))(c.wait_send)
     for step, _, c, _ in tall:
         c.wait_send()
         core_copy(2, 0, step, core).wait_send()
@@ -620,8 +661,8 @@
     ]
     for shape, column in (
         ((2, 2, 4, 4, 2), (2, 2, 2, 4, 4)),
-        ((2, 2, 4, 4, 2), (2, 2, 2, 4, 4)),
         ((2, 4, 4, 2), (2, 2, 4, 4)),
+        ((4, 4, 2), (2, 4, 4)),
         ((2, 4, 4, 2), (2, 2, 4, 4)),
         ((2, 3, 4, 2), (3, 4, 4)),
         ((2, 4, 2), (4, 4)),
@@ -651,7 +692,7 @@
         pltpu.VMEM((2, 2, 8, 16, 128), BF16),
         pltpu.VMEM((2, 2, 8, 16, 128), BF16),
     ]
-    for shape in ((3, 3, 3, 2), (3, 2, 4), (3, 3, 3, 2), (3, 2), (10,)):
+    for shape in ((3, 3, 3, 2), (3, 2, 4), (3, 3, 3, 3), (3, 2), (10,)):
         scratch += [pltpu.SemaphoreType.DMA(shape)] * 2
     scratch += [pltpu.SemaphoreType.DMA((5,)), pltpu.SemaphoreType.REGULAR((2,))]
     coarse_grad, summed = pl.pallas_call(

time: 63.9 us -> 61.7 us (0.966)
  Pallas kernels: 60.8 us -> 58.4 us
    pallas_call x1, Pallas kernels: 60.8 us -> 58.4 us  [body(): pl.pallas_call(kernel, out_shape=(jax.ShapeDtypeStruct((128, 256), BF16),...]
where the time goes in v4:
time: 61.7 us; the launch traced here: 61.3 us
  Pallas kernels  58.4 us (95%)
  other arithmetic  1.53 us (2%)
  between operations  0.7 us (1%)
  local copies, waits for them, and re-layouts  0.65 us (1%)
    pallas_call x1, Pallas kernels, body(): pl.pallas_call(kernel, out_shape=(jax.ShapeDtypeStruct((128, 256), BF16),...  58.4 us
    sub x1, other arithmetic, body(): new_master = master - learn_rate * corrected / scaled  1.53 us

profile of v4, /device:TPU:0, one launch (start us, length us, event | category | flops | bytes accessed | tf_op | source)
XLA Modules:
  0.0 61.3 jit_solution(2887310129167887176)
XLA Ops:
  0.6 0.0 copy-start
  0.6 0.0 copy-start.2
  0.7 0.0 copy-start.3
  0.7 58.4 %shard_map.102 = (bf16[128,256]{1,0:T(8,128)(2,1)}, f32[108,128]{1,0:T(8,128)}) custom-call(f32[108,128]{1,0:T(8,128)} %master_in.1, bf16[2,4,8,16,128]{4,3,2,1,0:T(8,128)(2,1)} %bitcast.5, bf16[2,4,8,16,128]{4,3,2,1,0:T(8,128)(2,1)} %bitcast.6, bf16[2,4,8,16,128]{4,3,2,1,0:T(8,128)(2,1)} %bitcast.7, bf16[2,2,32,256]{3,2,1,0:T(8,128)(2,1)} %bitcast.8), custom_call_target="tpu_custom_call" | custom-call | tf_op jit(solution)/shard_map/pallas_call | solution.py:698
  59.1 0.0 copy-done
  59.1 0.0 copy-done.2
  59.1 0.0 copy-done.3
  59.1 0.0 copy-start.1
  59.2 1.5 %divide_subtract_fusion = (f32[108,128]{1,0:T(8,128)}, f32[108,128]{1,0:T(8,128)}, f32[108,128]{1,0:T(8,128)}) fusion(f32[108,128]{1,0:T(8,128)S(1)} %copy-done, f32[108,128]{1,0:T(8,128)} %get-tuple-element.7, f32[108,128]{1,0:T(8,128)S(1)} %copy-done.2, f32[108,128]{1,0:T(8,128)S(1)} %copy-done.3), kind=kLoop, calls=%fused_computation | loop fusion | flops 179712 | bytes 387072 | tf_op jit(solution)/shard_map/sub | solution.py:722
  60.7 0.0 copy-done.1
  60.7 0.6 %copy.12 = bf16[1,2,2,4,8,256]{5,4,3,2,1,0:T(8,128)(2,1)} copy(bf16[1,2,2,4,8,256]{5,4,3,2,1,0:T(8,128)(2,1)S(1)} %bitcast.9) | data formatting | bytes 131072
Async XLA Ops:
  0.6 58.5 %copy-start = (f32[108,128]{1,0:T(8,128)S(1)}, f32[108,128]{1,0:T(8,128)}, u32[]{:S(2)}) copy-start(f32[108,128]{1,0:T(8,128)} %master_in.1) | copy-start | bytes 165892
  0.6 58.5 %copy-start.2 = (f32[108,128]{1,0:T(8,128)S(1)}, f32[108,128]{1,0:T(8,128)}, u32[]{:S(2)}) copy-start(f32[108,128]{1,0:T(8,128)} %param.12) | copy-start | bytes 165892
  0.7 58.5 %copy-start.3 = (f32[108,128]{1,0:T(8,128)S(1)}, f32[108,128]{1,0:T(8,128)}, u32[]{:S(2)}) copy-start(f32[108,128]{1,0:T(8,128)} %param.13) | copy-start | bytes 165892
  59.1 1.5 %copy-start.1 = (bf16[128,256]{1,0:T(8,128)(2,1)S(1)}, bf16[128,256]{1,0:T(8,128)(2,1)}, u32[]{:S(2)}) copy-start(bf16[128,256]{1,0:T(8,128)(2,1)} %get-tuple-element.6) | copy-start | bytes 196612

commit v5 on v4

--- a/solution.py
+++ b/solution.py
@@ -463,6 +463,9 @@
         third.append(gather(part, 2, LATE))
         go(core_copy(part, LATE, 0, core))
     tall_start(LATE)
+    wait_for(halos[2:])
+    pair = go(copy(coarse.at[0], coarse.at[1], halo_send.at[8], halo_recv.at[8], partner))
+    transposed_edges(act_up, halo_up)
     core_copy(2, EARLY, 0, other).wait_recv()
     tall_partner(EARLY)
     for part in range(2):
@@ -478,8 +481,11 @@
             keep = pre_mid[:, layer].reshape(256, 128).astype(F32) > 0.0
             value = jnp.where(keep, value, 0.0).astype(BF16)
             mid_raw[:, layer] = value.reshape(2, 8, 16, 128)
+
+    def widen_mid(layers):
+        for layer in layers:
             for sample in range(2):
-                widen(x_mid, sample, layer + 1, value[sample * 128 : sample * 128 + 128].astype(F32))
+                widen(x_mid, sample, layer + 1, mid_raw[sample, layer].reshape(128, 128).astype(F32))
 
     mid_layers((3, 0))
     mid_up = go(copy(mid_raw.at[:, 3], halo_mid.at[0], halo_send.at[0], halo_recv.at[0], after))
@@ -487,11 +493,9 @@
     core_sums(2, two_swap)
     early_sends(2)
     mid_layers((1, 2))
+    widen_mid((0, 1, 2, 3))
     lax.fori_loop(0, 16, unpack, 0)
     taps(w_one, 0, 128)
-    wait_for(halos[2:])
-    pair = go(copy(coarse.at[0], coarse.at[1], halo_send.at[8], halo_recv.at[8], partner))
-    transposed_edges(act_up, halo_up)
     for depth in range(3):
         grad_by_act(x_mid, act_up, 0, depth)
     lax.fori_loop(0, 16, pack, 0)
@@ -647,6 +651,18 @@
     for step, _, c, _ in tall:
         c.wait_send()
         core_copy(2, 0, step, core).wait_send()
+
+
+def finish(coarse, summed, master, moment, second, coarse_grad, new_master, new_moment, new_second):
+    coarse_grad[...] = coarse[...].astype(F32).reshape(coarse_grad.shape).astype(BF16)
+    mean_grad = summed[...] / 8.0
+    first = beta_one * moment[...] + (1.0 - beta_one) * mean_grad
+    squared = beta_two * second[...] + (1.0 - beta_two) * mean_grad * mean_grad
+    corrected = first / (1.0 - beta_one**adam_step)
+    scaled = jnp.sqrt(squared / (1.0 - beta_two**adam_step)) + adam_eps
+    new_moment[...] = first
+    new_second[...] = squared
+    new_master[...] = master[...] - learn_rate * corrected / scaled
 
 
 def body(coarse_in, pre_up, pre_mid, grad_out, master, moment, second):
@@ -714,13 +730,16 @@
         pre_up.reshape(pre_up.shape[1:]),
         coarse_in.reshape(2, 2, 32, 256),
     )
-    mean_grad = summed / 8.0
-    new_moment = beta_one * moment + (1.0 - beta_one) * mean_grad
-    new_second = beta_two * second + (1.0 - beta_two) * mean_grad * mean_grad
-    corrected = new_moment / (1.0 - beta_one**adam_step)
-    scaled = jnp.sqrt(new_second / (1.0 - beta_two**adam_step)) + adam_eps
-    new_master = master - learn_rate * corrected / scaled
-    return (coarse_grad.reshape(coarse_in.shape), new_master, new_moment, new_second)
+    coarse_shape = jax.ShapeDtypeStruct(coarse_in.shape, BF16)
+    rows_shape = jax.ShapeDtypeStruct((ROWS, 128), F32)
+    return tuple(
+        pl.pallas_call(
+            finish,
+            out_shape=(coarse_shape, rows_shape, rows_shape, rows_shape),
+            in_specs=[vmem] * 5,
+            out_specs=(vmem,) * 4,
+        )(coarse_grad, summed, master, moment, second)
+    )
 
 
 def solution(mesh):

time: 61.7 us -> 61.1 us (level)
  Pallas kernels: 58.4 us -> 60 us
  other arithmetic: 1.53 us -> 0 us
  local copies, waits for them, and re-layouts: 0.65 us -> 0 us
    pallas_call x0 -> x1, Pallas kernels: none -> 1.64 us  [body(): pl.pallas_call(finish, out_shape=(coarse_shape, rows_shape, rows_shape, r...]
    sub x1 -> x0, other arithmetic: 1.53 us -> none  [body(): new_master = master - learn_rate * corrected / scaled]
    unnamed x9 -> x0, local copies, waits for them, and re-layouts: 0.65 us -> none
where the time goes in v5:
time: 61.1 us; the launch traced here: 60.7 us
  Pallas kernels  60 us (98%)
  between operations  0.64 us (1%)
    pallas_call x1, Pallas kernels, body(): pl.pallas_call(kernel, out_shape=(jax.ShapeDtypeStruct((128, 256), BF16),...  58.4 us
    pallas_call x1, Pallas kernels, body(): pl.pallas_call(finish, out_shape=(coarse_shape, rows_shape, rows_shape, r...  1.64 us

profile of v5, /device:TPU:0, one launch (start us, length us, event | category | flops | bytes accessed | tf_op | source)
XLA Modules:
  0.0 60.7 jit_solution(18170964180527584262)
XLA Ops:
  0.6 58.4 %shard_map.102 = (bf16[128,256]{1,0:T(8,128)(2,1)}, f32[108,128]{1,0:T(8,128)}) custom-call(f32[108,128]{1,0:T(8,128)} %master.1, bf16[2,4,8,16,128]{4,3,2,1,0:T(8,128)(2,1)} %bitcast.4, bf16[2,4,8,16,128]{4,3,2,1,0:T(8,128)(2,1)} %bitcast.5, bf16[2,4,8,16,128]{4,3,2,1,0:T(8,128)(2,1)} %bitcast.6, bf16[2,2,32,256]{3,2,1,0:T(8,128)(2,1)} %bitcast.7), custom_call_target="tpu_custom_call" | custom-call | tf_op jit(solution)/shard_map/pallas_call | solution.py:714
  59.0 1.6 %shard_map.103 = (bf16[1,2,2,4,8,256]{5,4,3,2,1,0:T(8,128)(2,1)}, f32[108,128]{1,0:T(8,128)}, f32[108,128]{1,0:T(8,128)}, f32[108,128]{1,0:T(8,128)}) custom-call(bf16[128,256]{1,0:T(8,128)(2,1)} %get-tuple-element.6.coarse, f32[108,128]{1,0:T(8,128)} %get-tuple-element.7.summed, f32[108,128]{1,0:T(8,128)} %master.1, f32[108,128]{1,0:T(8,128)} %moment.1, ...), custom_call_target="tpu_custom_call" | custom-call | tf_op jit(solution)/shard_map/pallas_call | solution.py:736

commit v6 on v5

--- a/solution.py
+++ b/solution.py
@@ -494,19 +494,19 @@
     early_sends(2)
     mid_layers((1, 2))
     widen_mid((0, 1, 2, 3))
-    lax.fori_loop(0, 16, unpack, 0)
-    taps(w_one, 0, 128)
     for depth in range(3):
         grad_by_act(x_mid, act_up, 0, depth)
     lax.fori_loop(0, 16, pack, 0)
     one_swap = swap(0)
+    lax.fori_loop(0, 16, unpack, 0)
+    taps(w_one, 0, 128)
+    core_sums(0, one_swap)
+    early_sends(0)
     tall_forward(LATE)
     for part in range(2):
         forward(part, LATE, third[part])
     mid_up.wait_recv()
     mid_down.wait_recv()
-    core_sums(0, one_swap)
-    early_sends(0)
     edges(x_mid, halo_mid)
 
     for layers in ((3, 0), (1, 2)):
@@ -595,7 +595,6 @@
     tall_partner(LATE)
     for part in range(2):
         wait_for([core_copy(part, LATE, number, other) for number in range(4)])
-    early_second = [second_sums(part, EARLY, early_first[part]) for part in range(2)]
     lax.fori_loop(32, 64, unpack, 0)
     taps(w_up, 2 * FILTER, 256)
     up_next.wait_recv()
@@ -610,8 +609,7 @@
             left = gathered[0:128, index * 384 : index * 384 + 384]
         acc = acc + nt(left, w_up[index])
     coarse_grad[...] = acc.astype(BF16)
-    for part in range(2):
-        third_sums(part, EARLY, early_second[part])
+    early_second = [second_sums(part, EARLY, early_first[part]) for part in range(2)]
 
     for which, _, c in column:
         pl.when(tall_half == (LATE if which == 2 else EARLY))(c.wait_recv)
@@ -627,6 +625,8 @@
     lax.fori_loop(0, 4, add_plane, 0)
     plane = scatter(2, 1, us[2], rcs[2], 0)
     late_second = [second_sums(part, LATE, late_first[part]) for part in range(2)]
+    for part in range(2):
+        third_sums(part, EARLY, early_second[part])
     wait_for(plane)
     total = us[2][at["x"]].astype(F32)
     for step in range(3):

time: 61.1 us -> 60.2 us (0.985)
  Pallas kernels: 60 us -> 59.2 us
    pallas_call x1, Pallas kernels: 58.4 us -> 57.6 us  [body(): pl.pallas_call(kernel, out_shape=(jax.ShapeDtypeStruct((128, 256), BF16),...]
where the time goes in v6:
time: 60.2 us; the launch traced here: 59.8 us
  Pallas kernels  59.2 us (98%)
  between operations  0.64 us (1%)
    pallas_call x1, Pallas kernels, body(): pl.pallas_call(kernel, out_shape=(jax.ShapeDtypeStruct((128, 256), BF16),...  57.6 us
    pallas_call x1, Pallas kernels, body(): pl.pallas_call(finish, out_shape=(coarse_shape, rows_shape, rows_shape, r...  1.64 us

profile of v6, /device:TPU:0, one launch (start us, length us, event | category | flops | bytes accessed | tf_op | source)
XLA Modules:
  0.0 59.8 jit_solution(16798575786405448673)
XLA Ops:
  0.6 57.6 %shard_map.102 = (bf16[128,256]{1,0:T(8,128)(2,1)}, f32[108,128]{1,0:T(8,128)}) custom-call(f32[108,128]{1,0:T(8,128)} %master.1, bf16[2,4,8,16,128]{4,3,2,1,0:T(8,128)(2,1)} %bitcast.4, bf16[2,4,8,16,128]{4,3,2,1,0:T(8,128)(2,1)} %bitcast.5, bf16[2,4,8,16,128]{4,3,2,1,0:T(8,128)(2,1)} %bitcast.6, bf16[2,2,32,256]{3,2,1,0:T(8,128)(2,1)} %bitcast.7), custom_call_target="tpu_custom_call" | custom-call | tf_op jit(solution)/shard_map/pallas_call | solution.py:714
  58.2 1.6 %shard_map.103 = (bf16[1,2,2,4,8,256]{5,4,3,2,1,0:T(8,128)(2,1)}, f32[108,128]{1,0:T(8,128)}, f32[108,128]{1,0:T(8,128)}, f32[108,128]{1,0:T(8,128)}) custom-call(bf16[128,256]{1,0:T(8,128)(2,1)} %get-tuple-element.6.coarse, f32[108,128]{1,0:T(8,128)} %get-tuple-element.7.summed, f32[108,128]{1,0:T(8,128)} %master.1, f32[108,128]{1,0:T(8,128)} %moment.1, ...), custom_call_target="tpu_custom_call" | custom-call | tf_op jit(solution)/shard_map/pallas_call | solution.py:736

commit v7 on v6

--- a/solution.py
+++ b/solution.py
@@ -403,11 +403,10 @@
                 pl.when(owner == EARLY)(c.start)
 
     def late_sends():
-        out = [scatter(part, 0, tot[part].at[LATE], ras[part].at[LATE], 2) for part in range(2)]
         for which, owner, c in column:
             if which == 2:
                 pl.when(owner == LATE)(c.start)
-        return out
+        return [scatter(part, 0, tot[part].at[LATE], ras[part].at[LATE], 2) for part in range(2)]
 
     for load in loads[1:]:
         load.wait()
@@ -505,68 +504,6 @@
     tall_forward(LATE)
     for part in range(2):
         forward(part, LATE, third[part])
-    mid_up.wait_recv()
-    mid_down.wait_recv()
-    edges(x_mid, halo_mid)
-
-    for layers in ((3, 0), (1, 2)):
-        both = back_conv(x_mid, w_one, layers)
-        for number, layer in enumerate(layers):
-            value = both[number * 256 : number * 256 + 256]
-            keep = pre_up[:, layer].reshape(256, 128).astype(F32) > 0.0
-            value = jnp.where(keep, value, 0.0).astype(BF16)
-            up_raw[0, :, layer] = value.reshape(2, 128, 128)
-    up_pair = go(copy(up_raw.at[0], up_raw.at[1], halo_send.at[2], halo_recv.at[2], partner))
-    up_next = go(copy(up_raw.at[0, :, 3], up_before, halo_send.at[9], halo_recv.at[9], after))
-
-    def second_sums(part, half, copies):
-        wait_for(copies)
-        mine = at[ORDER[part][2]]
-
-        def add(index, carry):
-            total = tot[part][half, mine, index].astype(F32)
-            for step in range(3):
-                total = total + ras[part][half, step, index].astype(F32)
-            us[part][half, index] = total.astype(BF16)
-            return carry
-
-        lax.fori_loop(0, 4, add, 0)
-        return scatter(part, 1, us[part].at[half], rcs[part].at[half], half)
-
-    def third_sums(part, half, copies):
-        wait_for(copies)
-        total = us[part][half, at[ORDER[part][1]]].astype(F32)
-        for step in range(3):
-            total = total + rcs[part][half, step].astype(F32)
-        vs[part][2 * half : 2 * half + 2] = total.astype(BF16)
-
-    pick_row = lax.broadcasted_iota(jnp.int32, (288, 128), 0)
-    pick_lane = lax.broadcasted_iota(jnp.int32, (288, 128), 1)
-    tap, coarse_row, coarse_col = pick_row // 32, lax.rem(pick_row // 8, 4), lax.rem(pick_row, 8)
-    fine_row = 2 * coarse_row + tap // 3 - 1
-    fine_col = 2 * coarse_col + lax.rem(tap, 3) - 1
-    chosen = (fine_row >= 0) & (fine_col >= 0) & (pick_lane == fine_row * 16 + fine_col)
-    pick = jnp.where(chosen, 1.0, 0.0).astype(BF16)
-
-    def spread(slot, sample, layer):
-        picked = nn(pick, up_raw[slot, sample, layer]).astype(BF16)
-        first = ((slot * 2 + sample) * 2 + layer // 2) * 32
-        for depth in (1,) if layer % 2 == 0 else (0, 2):
-            for tap in range(9):
-                columns = slice((depth * 9 + tap) * 128, (depth * 9 + tap) * 128 + 128)
-                gathered[first : first + 32, columns] = picked[tap * 32 : tap * 32 + 32]
-        return picked
-
-    def lower(sample, quarter, picked):
-        first = (sample * 2 + quarter) * 32
-        for tap in range(9):
-            lowest[first : first + 32, tap * 128 : tap * 128 + 128] = picked[tap * 32 : tap * 32 + 32]
-
-    for sample in range(2):
-        for layer in range(4):
-            picked = spread(0, sample, layer)
-            if layer == 1:
-                lower(sample, 1, picked)
     pair.wait_recv()
     turned = []
     for first in (1, 0):
@@ -579,7 +516,76 @@
                         value = jnp.where(slab < 31, value, 0.0)
                     rows.append(value)
         turned.append(jnp.concatenate(rows, axis=0).T.astype(BF16))
-    up_pair.wait_recv()
+    mid_up.wait_recv()
+    mid_down.wait_recv()
+    edges(x_mid, halo_mid)
+
+    up_pair = []
+    for layers in ((3, 0), (1, 2)):
+        both = back_conv(x_mid, w_one, layers)
+        for number, layer in enumerate(layers):
+            value = both[number * 256 : number * 256 + 256]
+            keep = pre_up[:, layer].reshape(256, 128).astype(F32) > 0.0
+            value = jnp.where(keep, value, 0.0).astype(BF16)
+            up_raw[0, :, layer] = value.reshape(2, 128, 128)
+        if layers[0] == 3:
+            up_next = go(copy(up_raw.at[0, :, 3], up_before, halo_send.at[9], halo_recv.at[9], after))
+            cuts = ((2, slice(3, 4)), (10, slice(0, 1)))
+        else:
+            cuts = ((11, slice(1, 3)),)
+        for sem, cut in cuts:
+            src, dst = up_raw.at[0, :, cut], up_raw.at[1, :, cut]
+            up_pair.append(go(copy(src, dst, halo_send.at[sem], halo_recv.at[sem], partner)))
+
+    def second_sums(part, half, copies):
+        wait_for(copies)
+        mine = at[ORDER[part][2]]
+
+        def add(index, carry):
+            total = tot[part][half, mine, index].astype(F32)
+            for step in range(3):
+                total = total + ras[part][half, step, index].astype(F32)
+            us[part][half, index] = total.astype(BF16)
+            return carry
+
+        lax.fori_loop(0, 4, add, 0)
+        return scatter(part, 1, us[part].at[half], rcs[part].at[half], half)
+
+    def third_sums(part, half, copies):
+        wait_for(copies)
+        total = us[part][half, at[ORDER[part][1]]].astype(F32)
+        for step in range(3):
+            total = total + rcs[part][half, step].astype(F32)
+        vs[part][2 * half : 2 * half + 2] = total.astype(BF16)
+
+    pick_row = lax.broadcasted_iota(jnp.int32, (288, 128), 0)
+    pick_lane = lax.broadcasted_iota(jnp.int32, (288, 128), 1)
+    tap, coarse_row, coarse_col = pick_row // 32, lax.rem(pick_row // 8, 4), lax.rem(pick_row, 8)
+    fine_row = 2 * coarse_row + tap // 3 - 1
+    fine_col = 2 * coarse_col + lax.rem(tap, 3) - 1
+    chosen = (fine_row >= 0) & (fine_col >= 0) & (pick_lane == fine_row * 16 + fine_col)
+    pick = jnp.where(chosen, 1.0, 0.0).astype(BF16)
+
+    def spread(slot, sample, layer):
+        picked = nn(pick, up_raw[slot, sample, layer]).astype(BF16)
+        first = ((slot * 2 + sample) * 2 + layer // 2) * 32
+        for depth in (1,) if layer % 2 == 0 else (0, 2):
+            for tap in range(9):
+                columns = slice((depth * 9 + tap) * 128, (depth * 9 + tap) * 128 + 128)
+                gathered[first : first + 32, columns] = picked[tap * 32 : tap * 32 + 32]
+        return picked
+
+    def lower(sample, quarter, picked):
+        first = (sample * 2 + quarter) * 32
+        for tap in range(9):
+            lowest[first : first + 32, tap * 128 : tap * 128 + 128] = picked[tap * 32 : tap * 32 + 32]
+
+    for sample in range(2):
+        for layer in range(4):
+            picked = spread(0, sample, layer)
+            if layer == 1:
+                lower(sample, 1, picked)
+    wait_for(up_pair)
     for sample in range(2):
         for layer in range(4):
             spread(1, sample, layer)
@@ -708,7 +714,7 @@
         pltpu.VMEM((2, 2, 8, 16, 128), BF16),
         pltpu.VMEM((2, 2, 8, 16, 128), BF16),
     ]
-    for shape in ((3, 3, 3, 2), (3, 2, 4), (3, 3, 3, 3), (3, 2), (10,)):
+    for shape in ((3, 3, 3, 2), (3, 2, 4), (3, 3, 3, 3), (3, 2), (12,)):
         scratch += [pltpu.SemaphoreType.DMA(shape)] * 2
     scratch += [pltpu.SemaphoreType.DMA((5,)), pltpu.SemaphoreType.REGULAR((2,))]
     coarse_grad, summed = pl.pallas_call(

time: 60.2 us -> 60.4 us (level)
  no operation moved by 1% of the time
where the time goes in v7:
time: 60.4 us; the launch traced here: 60 us
  Pallas kernels  59.4 us (98%)
  between operations  0.64 us (1%)
    pallas_call x1, Pallas kernels, body(): pl.pallas_call(kernel, out_shape=(jax.ShapeDtypeStruct((128, 256), BF16),...  57.8 us
    pallas_call x1, Pallas kernels, body(): pl.pallas_call(finish, out_shape=(coarse_shape, rows_shape, rows_shape, r...  1.64 us

profile of v7, /device:TPU:0, one launch (start us, length us, event | category | flops | bytes accessed | tf_op | source)
XLA Modules:
  0.0 60.0 jit_solution(3008736172615419078)
XLA Ops:
  0.6 57.8 %shard_map.102 = (bf16[128,256]{1,0:T(8,128)(2,1)}, f32[108,128]{1,0:T(8,128)}) custom-call(f32[108,128]{1,0:T(8,128)} %master.1, bf16[2,4,8,16,128]{4,3,2,1,0:T(8,128)(2,1)} %bitcast.4, bf16[2,4,8,16,128]{4,3,2,1,0:T(8,128)(2,1)} %bitcast.5, bf16[2,4,8,16,128]{4,3,2,1,0:T(8,128)(2,1)} %bitcast.6, bf16[2,2,32,256]{3,2,1,0:T(8,128)(2,1)} %bitcast.7), custom_call_target="tpu_custom_call" | custom-call | tf_op jit(solution)/shard_map/pallas_call | solution.py:720
  58.4 1.6 %shard_map.103 = (bf16[1,2,2,4,8,256]{5,4,3,2,1,0:T(8,128)(2,1)}, f32[108,128]{1,0:T(8,128)}, f32[108,128]{1,0:T(8,128)}, f32[108,128]{1,0:T(8,128)}) custom-call(bf16[128,256]{1,0:T(8,128)(2,1)} %get-tuple-element.6.coarse, f32[108,128]{1,0:T(8,128)} %get-tuple-element.7.summed, f32[108,128]{1,0:T(8,128)} %master.1, f32[108,128]{1,0:T(8,128)} %moment.1, ...), custom_call_target="tpu_custom_call" | custom-call | tf_op jit(solution)/shard_map/pallas_call | solution.py:742
